TPU v7x, 256 devices: a whole 4x4x8 slice. The times are simulated.
256 devices in a mesh: rep: 128 (over z, y, x), feat: 2 (over core).
Axes of the slice: x: 4, y: 4, z: 8, core: 2. Of those that a mesh axis runs over, the one named last changes fastest.
Arguments:
- rows: bfloat16 [65536, 768], P('rep', 'feat'), may hold values from -6 to 6
- list_ids: int32 [65536], P('rep'), may hold values from 0 to 16383, as said below
- code_ids: int32 [65536], P('rep'), may hold values from 0 to 4095, as said below
- list_slot: int32 [16384], replicated, may hold values from 0 to 16383, as said below
- coarse: bfloat16 [16384, 768], P('rep'), may hold values from -6 to 6
- codebook: float32 [4096, 768], P(('rep', 'feat')), may hold values from -6 to 6
Outputs:
- updated_codebook: float32 [4096, 768], P(('rep', 'feat'))
- nearest: float32 [65536], P('rep')
Inputs may be any that keep to these rules, and one draw needn't show every extreme that they name: A permutation: every slot holds one list; the owner of a list is list_slot // 128. `list_ids`: among the 512 rows of one device, the lists of one owner are named at most 8 times, and exactly 8 times for some owner. `code_ids`: take an owner r of lists and a half f (0 or 1) of the indices of rep; the rows of the devices with rep index in [f * 64, (f + 1) * 64) whose lists r owns name the codewords of any group g (codewords g * 16 up to the next group) at most 2 times, and exactly 2 times for some r, f and g.
All inputs are finite; a program needn't handle non-finite values.
Results may differ from a plain program's by a relative error of at most 0.0013.
The roundings to bfloat16 on the way count: a program that leaves them out, or rounds other values in their place, can miss the bound.
Values may be sent and summed in bfloat16 or wider, within the bound.
A program may use at most 64 MiB of HBM per device.

v0:
```python
import jax
import jax.numpy as jnp
from jax import lax
from jax.sharding import PartitionSpec as P

FEATURES = 768
CODES = 4096


prior_weight = 8.0


def per_device(rows, list_ids, code_ids, list_slot, coarse, codebook):
    peers = lax.axis_size("rep")
    half_peers = peers // 2
    row_count = rows.shape[0]
    capacity = 2 * row_count // peers
    lists_here = coarse.shape[0]
    slot = jnp.take(list_slot, list_ids)
    target = slot // lists_here
    local_list = slot - target * lists_here
    owners = (target[:, None] == jnp.arange(peers, dtype=jnp.int32)[None, :]).astype(jnp.int32)
    place = jnp.sum(jnp.cumsum(owners, axis=0) * owners, axis=1) - 1
    flat = target * capacity + place
    labels = jnp.stack([local_list, code_ids], axis=1)
    packed_meta = (
        jnp.full((peers * capacity, 2), -1, jnp.int32)
        .at[flat]
        .set(labels)
        .reshape(peers, capacity, 2)
    )
    whole = lax.all_gather(rows, "feat", axis=1, tiled=True)
    packed = jnp.zeros((peers * capacity, whole.shape[1]), jnp.bfloat16).at[flat].set(whole)
    packed = packed.reshape(peers, capacity, whole.shape[1])
    every, every_meta = (
        lax.all_to_all(packed, "rep", split_axis=0, concat_axis=0, tiled=True),
        lax.all_to_all(packed_meta, "rep", split_axis=0, concat_axis=0, tiled=True),
    )
    offset = lax.axis_index("feat") * half_peers
    arrived = lax.dynamic_slice_in_dim(every, offset, half_peers, 0)
    meta = lax.dynamic_slice_in_dim(every_meta, offset, half_peers, 0)
    width = arrived.shape[2]
    lists_got = jnp.maximum(meta[:, :, 0].reshape(-1), 0)
    codes_got = meta[:, :, 1].reshape(-1)
    residual = arrived.reshape(-1, width).astype(jnp.float32) - jnp.take(
        coarse, lists_got, axis=0
    ).astype(jnp.float32)
    res_b = residual.astype(jnp.bfloat16)
    code_hits = (codes_got[:, None] == jnp.arange(CODES, dtype=jnp.int32)[None, :]).astype(
        jnp.bfloat16
    )
    partial_sums = lax.dot_general(
        code_hits, res_b, (((0,), (0,)), ((), ())), preferred_element_type=jnp.float32
    )
    partial_counts = jnp.sum(code_hits, axis=0, dtype=jnp.float32)
    sums, counts = (
        lax.psum_scatter(partial_sums, ("rep", "feat"), scatter_dimension=0, tiled=True),
        lax.psum_scatter(partial_counts, ("rep", "feat"), scatter_dimension=0, tiled=True),
    )
    updated = (sums + prior_weight * codebook) / (counts[:, None] + prior_weight)
    row_norm = jnp.sum(jnp.square(res_b.astype(jnp.float32)), axis=1)
    initial = jnp.full((res_b.shape[0],), 3e38, jnp.float32)
    book_piece = updated.astype(jnp.bfloat16)
    piece = lax.all_gather(book_piece, ("rep", "feat"), axis=0, tiled=True)
    dots = lax.dot_general(
        res_b, piece, (((1,), (1,)), ((), ())), preferred_element_type=jnp.float32
    )
    book_norm = jnp.sum(jnp.square(piece.astype(jnp.float32)), axis=1)
    dist = (row_norm[:, None] - 2.0 * dots + book_norm[None, :]) / FEATURES
    best = jnp.minimum(initial, jnp.min(dist, axis=1))
    mins_half = best.reshape(half_peers, capacity)
    mins_all = lax.all_gather(mins_half, "feat", axis=0, tiled=True)
    returned = lax.all_to_all(mins_all, "rep", split_axis=0, concat_axis=0, tiled=True)
    nearest = jnp.take(returned.reshape(-1), flat)
    return (updated, nearest)


def solution(mesh):
    placed = (P("rep", "feat"), P("rep"), P("rep"), P(), P("rep", None), P(("rep", "feat"), None))
    return jax.shard_map(
        per_device,
        mesh=mesh,
        in_specs=placed,
        out_specs=(P(("rep", "feat"), None), P("rep")),
        check_vma=False,
    )
```

profile of v0, /device:TPU:1, one launch (start us, length us, event | category | flops | bytes accessed | tf_op | source)
XLA Modules:
  0.0 664.3 jit_solution(14675981654192083993)
XLA Ops:
  7.2 0.7 compare_select_fusion.1
  7.9 3.5 gather_fusion
  11.6 0.2 fusion.9
  11.9 0.2 fusion.8
  12.4 1.8 scatter_custom_fusion
  14.2 1.5 copy.38
  15.7 16.3 %all-to-all-start = ((s32[128,8,2]{1,2,0:T(2,128)}), s32[128,8,2]{1,2,0:T(2,128)S(1)}, u32[]{:S(2)}, u32[]{:S(2)}) async-start(s32[128,8,2]{1,2,0:T(2,128)} %copy.38), calls=%async_computation | async-start | bytes 262144 | tf_op jit(solution)/shard_map/all_to_all | solution.py:37
  32.0 3.0 all_gather.9
  35.0 3.8 scatter_custom_fusion.1
  38.8 4.5 all-to-all-done
  43.2 9.0 %all-to-all-start.1 = ((bf16[128,8,768]{2,1,0:T(8,128)(2,1)}), bf16[128,8,768]{2,1,0:T(8,128)(2,1)S(1)}, u32[]{:S(2)}, u32[]{:S(2)}) async-start(bf16[128,8,768]{2,1,0:T(8,128)(2,1)} %bitcast.7), calls=%async_computation.1 | async-start | bytes 3145728 | tf_op jit(solution)/shard_map/all_to_all | solution.py:36
  52.2 0.2 reduce-scatter.2.cloned.1.call-start
  53.2 2.0 gather_fusion.1
  55.2 36.8 %all-to-all-done.1 = bf16[128,8,768]{2,1,0:T(8,128)(2,1)S(1)} async-done(((bf16[128,8,768]{2,1,0:T(8,128)(2,1)}), bf16[128,8,768]{2,1,0:T(8,128)(2,1)S(1)}, u32[]{:S(2)}, u32[]{:S(2)}) %all-to-all-start.1) | async-done | bytes 1572896 | tf_op jit(solution)/shard_map/all_to_all | solution.py:36
  92.0 6.8 %fusion.1 = f32[4096,768]{1,0:T(8,128)} fusion(s32[512]{0:T(512)S(1)} %eq.45, bf16[512,768]{1,0:T(8,128)(2,1)S(1)} %gather_fusion.1, pred[512]{0:T(512)(128)(4,1)S(1)} %le.39, bf16[128,8,768]{2,1,0:T(8,128)(2,1)S(1)} %all-to-all-done.1, s32[]{:T(128)S(6)} %select_n.59), kind=kOutput, calls=%fused_computation.10 | convolution fusion | flops 3225288704 | bytes 14158340 | tf_op jit(solution)/shard_map/dot_general | solution.py:52
  98.9 2.0 convert_reduce_fusion
  100.9 75.4 %all-reduce = f32[4096]{0:T(1024)S(1)} all-reduce(f32[4096]{0:T(1024)S(1)} %convert_reduce_fusion), channel_id=3, replica_groups=mesh['rep'=128,'feat'=2] {'rep','feat'}, use_global_device_ids=true, to_apply=%region_7.8.clone | all-reduce | flops 4096 | bytes 32768
  176.4 322.0 %reduce-scatter.2.cloned.1.call-done = f32[16,768]{1,0:T(8,128)} async-done(((f32[4096,768]{1,0:T(8,128)}), f32[16,768]{1,0:T(8,128)}) %reduce-scatter.2.cloned.1.call-update) | async-done | bytes 49168 | tf_op jit(solution)/shard_map/reduce_scatter | solution.py:57
  498.4 1.5 fusion.18
  500.0 0.5 multiply_reduce_fusion.2
  500.6 120.3 %all-gather.3.cloned.1.call-done = bf16[4096,768]{1,0:T(8,128)(2,1)} async-done(((bf16[16,768]{1,0:T(8,128)(2,1)}), bf16[4096,768]{1,0:T(8,128)(2,1)}) %all-gather.3.cloned.1.call-update) | async-done | bytes 6291472 | tf_op jit(solution)/shard_map/all_gather | solution.py:64
  620.9 4.2 multiply_reduce_fusion
  625.1 0.4 copy-done.1
  625.5 4.2 multiply_reduce_fusion.1
  629.8 1.8 all-gather
  631.6 0.7 copy.49
  632.3 10.0 %all-to-all-start.2 = ((f32[128,1,8]{2,1,0:T(1,128)}), f32[128,1,8]{2,1,0:T(1,128)S(1)}, u32[]{:S(2)}, u32[]{:S(2)}) async-start(f32[128,1,8]{2,1,0:T(1,128)} %bitcast.11), calls=%async_computation.3 | async-start | bytes 131072 | tf_op jit(solution)/shard_map/all_to_all | solution.py:73
  642.4 10.7 %all-to-all-done.2 = f32[128,1,8]{2,1,0:T(1,128)S(1)} async-done(((f32[128,1,8]{2,1,0:T(1,128)}), f32[128,1,8]{2,1,0:T(1,128)S(1)}, u32[]{:S(2)}, u32[]{:S(2)}) %all-to-all-start.2) | async-done | bytes 4128 | tf_op jit(solution)/shard_map/all_to_all | solution.py:73
  653.1 0.5 broadcast.170
  653.6 0.8 reduce.7
  654.5 2.3 gather_fusion.2
  656.8 0.6 and_select_fusion
  (45 shorter events, 1.7 us)
Async XLA Ops:
  7.2 46.0 %copy-start = (bf16[128,768]{1,0:T(8,128)(2,1)S(1)}, bf16[128,768]{1,0:T(8,128)(2,1)}, u32[]{:S(2)}) copy-start(bf16[128,768]{1,0:T(8,128)(2,1)} %param.10) | copy-start | bytes 589828
  7.2 4.3 copy-start.4
  7.2 5.0 copy-start.5
  11.5 20.5 %copy-start.2 = (bf16[512,384]{1,0:T(8,128)(2,1)S(1)}, bf16[512,384]{1,0:T(8,128)(2,1)}, u32[]{:S(2)}) copy-start(bf16[512,384]{1,0:T(8,128)(2,1)} %param.6) | copy-start | bytes 1179652
  15.7 27.6 %all-to-all-start = ((s32[128,8,2]{1,2,0:T(2,128)}), s32[128,8,2]{1,2,0:T(2,128)S(1)}, u32[]{:S(2)}, u32[]{:S(2)}) async-start(s32[128,8,2]{1,2,0:T(2,128)} %copy.38), calls=%async_computation | async-start | bytes 262144 | tf_op jit(solution)/shard_map/all_to_all | solution.py:37
  43.2 48.8 %all-to-all-start.1 = ((bf16[128,8,768]{2,1,0:T(8,128)(2,1)}), bf16[128,8,768]{2,1,0:T(8,128)(2,1)S(1)}, u32[]{:S(2)}, u32[]{:S(2)}) async-start(bf16[128,8,768]{2,1,0:T(8,128)(2,1)} %bitcast.7), calls=%async_computation.1 | async-start | bytes 3145728 | tf_op jit(solution)/shard_map/all_to_all | solution.py:36
  52.2 446.1 %reduce-scatter.2.cloned.1.call-start = ((), (), s32[]{:S(2)}) async-start(), calls=%async_computation.4 | async-start | bytes 12632064 | tf_op jit(solution)/shard_map/reduce_scatter | solution.py:57
  98.8 399.5 %copy-start.3 = (f32[16,768]{1,0:T(8,128)S(1)}, f32[16,768]{1,0:T(8,128)}, u32[]{:S(2)}) copy-start(f32[16,768]{1,0:T(8,128)} %param.11) | copy-start | bytes 147460
  98.9 522.0 %all-gather.3.cloned.1.call-start = ((), (), s32[]{:S(2)}) async-start(), calls=%async_computation.5 | async-start | bytes 6316032 | tf_op jit(solution)/shard_map/all_gather | solution.py:64
  620.9 4.6 copy-start.1
  632.3 20.8 %all-to-all-start.2 = ((f32[128,1,8]{2,1,0:T(1,128)}), f32[128,1,8]{2,1,0:T(1,128)S(1)}, u32[]{:S(2)}, u32[]{:S(2)}) async-start(f32[128,1,8]{2,1,0:T(1,128)} %bitcast.11), calls=%async_computation.3 | async-start | bytes 131072 | tf_op jit(solution)/shard_map/all_to_all | solution.py:73
Sparse Core Ops, SparseCore 0:
  99.0 399.3 reduce-scatter.1
  502.1 118.7 all-gather.2
where the time goes:
time: 665 us; the launch traced here: 664 us
  waiting for transfers between devices  494 us (74%)
  blocking collectives  80.1 us (12%)
  starting transfers between devices  35.7 us (5%)
  local copies, waits for them, and re-layouts  17.9 us (3%)
  between operations  14.3 us (2%)
  other arithmetic  11 us (2%)
  matrix products  11 us (2%)
    reduce_scatter x1, waiting for transfers between devices, per_device(): lax.psum_scatter(partial_sums, ('rep', 'feat'), scatter_dimension=0, tile...  322 us
    all_gather x1, waiting for transfers between devices, per_device(): piece = lax.all_gather(book_piece, ('rep', 'feat'), axis=0, tiled=True)  120 us
    unnamed x1, blocking collectives  75.4 us
    all_to_all x1, waiting for transfers between devices, per_device(): lax.all_to_all(packed, 'rep', split_axis=0, concat_axis=0, tiled=True)  36.8 us
    all_to_all x1, starting transfers between devices, per_device(): lax.all_to_all(packed_meta, 'rep', split_axis=0, concat_axis=0, tiled=True)  16.3 us
  transfers between devices with their start and end apart: 5, of which 5 were waited for; matrix products, arithmetic and copies ran while one was open for 1% of the time, Pallas kernels for 0%

commit v1 on v0

v1 whole, which is shorter than its diff:
```python
import jax
import jax.numpy as jnp
from jax import lax
from jax.experimental import pallas as pl
from jax.experimental.pallas import tpu as pltpu
from jax.sharding import PartitionSpec as P

NZ, NY, NX = 8, 4, 4
CHIPS = NZ * NY * NX
FEATURES = 768
HALF = FEATURES // 2
ROWS = 512
CAP = 8
SLOTS = CHIPS * CAP
PRIOR = 8.0
MESH = pl.DeviceIdType.MESH
F32, BF16, I32 = jnp.float32, jnp.bfloat16, jnp.int32
PLANE = NY * NX
CHUNK = PLANE * CAP

ORDERS = ("xyz", "yzx", "zxy")
PART = FEATURES // 3


def iota(shape, axis):
    return lax.broadcasted_iota(I32, shape, axis)


def one_hot(mask):
    return jnp.where(mask, 1.0, 0.0).astype(BF16)


def dot(a, b, over=((1,), (0,))):
    return lax.dot_general(a, b, (over, ((), ())), preferred_element_type=F32)


def split3(v):
    a = v.astype(BF16)
    r = v - a.astype(F32)
    b = r.astype(BF16)
    return a, b, (r - b.astype(F32)).astype(BF16)


def to_message(v):
    v = v.reshape(PLANE, CAP, 2 * PART)
    return jnp.concatenate([v[:, :, :PART], v[:, :, PART:]], axis=1).astype(BF16)


def from_message(m):
    m = m.astype(F32)
    top = m[:, :CAP, :].reshape(CHUNK, PART)
    low = m[:, CAP:, :].reshape(CHUNK, PART)
    return jnp.concatenate([top, low[:, :128]], axis=1), low[:, 128:]


def kernel(
    rows_ref, lid_ref, code_ref, table_ref, coarse_ref, codebook_ref,
    updated_ref, nearest_ref,
    rows_ext, send_a, recv_a, send_b, recv_b, res_ext, res_full, row_rhs,
    sums_own, sums_sib, book_x, book_y, book_z, min_send, min_recv, near_own, near_sib,
    a_send, a_recv, b_send, b_recv, e_send, e_recv, g_send, g_recv, p_send, p_recv,
):
    rep, feat = lax.axis_index("rep"), lax.axis_index("feat")
    z, y, x = rep // PLANE, rep // NX % NY, rep % NX

    def chip(dz, dy, dx):
        return (z + dz) % NZ * PLANE + (y + dy) % NY * NX + (x + dx) % NX

    def ahead(s):
        return (chip(s // PLANE, s // NX % NY, s % NX), feat)

    def behind(s):
        return (chip(NZ - s // PLANE, NY - s // NX % NY, NX - s % NX), feat)

    def nth(i):
        return i % NZ * PLANE + i // NZ

    sibling = (rep, 1 - feat)

    barrier = pltpu.get_barrier_semaphore()

    def greet(s, carry):
        pl.semaphore_signal(barrier, inc=1, device_id=ahead(s), device_id_type=MESH)
        return carry

    lax.fori_loop(1, CHIPS, greet, 0)
    pl.semaphore_signal(barrier, inc=1, device_id=sibling, device_id_type=MESH)

    lid, code = lid_ref[...], code_ref[...]
    table = table_ref[...]
    high = one_hot(iota((128, ROWS), 0) == (lid >> 7))
    low = iota((128, ROWS), 0) == (lid & 127)

    def look_up(t):
        got = dot(t.astype(F32).astype(BF16), high, ((0,), (0,)))
        return jnp.sum(jnp.where(low, got, 0.0), axis=0, keepdims=True)

    owner, local = look_up(table >> 7), look_up(table & 127)
    owner_i = owner.astype(I32)
    rel = (
        (((owner_i >> 4) - z) & (NZ - 1)) * PLANE
        + (((owner_i >> 2) - y) & (NY - 1)) * NX
        + ((owner_i - x) & (NX - 1))
    )
    line = iota((16, ROWS), 0)
    labels = jnp.where(line == 0, local + 1.0, 0.0)
    labels = jnp.where(line == 1, ((code >> 6) + 1).astype(F32), labels)
    labels = jnp.where(line == 2, (code & 63).astype(F32), labels)
    labels = jnp.where(line == 3, owner, labels)
    eye = one_hot(iota((16, 128), 0) == iota((16, 128), 1))
    labels = dot(labels.astype(BF16), eye, ((0,), (0,)))
    rows_ext[:, :HALF] = rows_ref[...]
    rows_ext[:, HALF:] = labels.astype(BF16)
    same = (labels[:, 3:4] == owner) & (iota((ROWS, ROWS), 0) < iota((ROWS, ROWS), 1))
    rank = jnp.sum(jnp.where(same, 1.0, 0.0), axis=0, keepdims=True).astype(I32)
    dest = rel * CAP + rank

    def pack_rows(c, carry):
        pick = one_hot(iota((CHUNK, ROWS), 0) + c * CHUNK == dest)
        send_a[pl.ds(c * PLANE, PLANE)] = to_message(dot(pick, rows_ext[...]))
        return carry

    lax.fori_loop(0, NZ, pack_rows, 0)

    pl.semaphore_wait(barrier, CHIPS)

    def exchange(src, dst, send_sem, recv_sem):
        def start(i, carry):
            s = nth(i)
            pltpu.make_async_remote_copy(
                src_ref=src.at[s], dst_ref=dst.at[s], send_sem=send_sem, recv_sem=recv_sem,
                device_id=ahead(s), device_id_type=MESH,
            ).start()
            return carry

        lax.fori_loop(1, CHIPS, start, 0)
        dst[0] = src[0]

    def others(buf, sem):
        return pltpu.make_async_copy(buf.at[pl.ds(1, CHIPS - 1)], buf.at[pl.ds(1, CHIPS - 1)], sem)

    exchange(send_a, recv_a, a_send, a_recv)
    others(recv_a, a_recv).wait()

    eye_t = eye

    def residuals(c, carry):
        v, tags = from_message(recv_a[pl.ds(c * PLANE, PLANE)])
        pick = one_hot(iota((CHUNK, 128), 1) + 1 == tags[:, 0:1].astype(I32))
        base = dot(pick, coarse_ref[:, pl.ds(pl.multiple_of(feat * HALF, 128), HALF)])
        res = (v - base).astype(BF16)
        at = pl.ds(c * CHUNK, CHUNK)
        res_ext[at, :HALF] = res
        res_ext[at, HALF:] = tags.astype(BF16)
        res_full[feat, at, :] = res
        return carry

    lax.fori_loop(0, NZ, residuals, 0)
    swap_res = pltpu.make_async_remote_copy(
        src_ref=res_full.at[feat], dst_ref=res_full.at[feat], send_sem=p_send.at[0],
        recv_sem=p_recv.at[0], device_id=sibling, device_id_type=MESH,
    )
    swap_res.start()

    tags_t = dot(eye_t, res_ext[:, HALF:], ((1,), (1,)))
    code_i = ((tags_t[1:2] - 1.0) * 64.0 + tags_t[2:3]).astype(I32)
    src_z = (z - iota((1, SLOTS), 1) // CHUNK) & (NZ - 1)
    half = src_z >> 2
    key = jnp.where(code_i >= 0, (code_i >> 4) * 2 + half, -1).astype(F32)

    def count(c, carry):
        at = pl.ds(c * CHUNK, CHUNK)
        tags = res_ext[at, HALF:].astype(F32)
        code_c = ((tags[:, 1:2] - 1.0) * 64.0 + tags[:, 2:3]).astype(I32)
        key_c = ((code_c >> 4) * 2 + (((z - c) & (NZ - 1)) >> 2)).astype(F32)
        before = iota((CHUNK, SLOTS), 0) + c * CHUNK < iota((CHUNK, SLOTS), 1)
        hit = jnp.where((key_c == key) & before, 1.0, 0.0)
        return carry + jnp.sum(hit, axis=0, keepdims=True)

    rank_b = lax.fori_loop(0, NZ, count, jnp.zeros((1, SLOTS), F32)).astype(I32)
    home = code_i >> 5
    rel_b = (
        (((home >> 4) - z) & (NZ - 1)) * PLANE
        + (((home >> 2) - y) & (NY - 1)) * NX
        + ((home - x) & (NX - 1))
    )
    dest_b = rel_b * CAP + ((code_i >> 4) & 1) * 4 + half * 2 + rank_b
    dest_b = jnp.where(code_i >= 0, dest_b, -1)

    def pack_res(c, carry):
        pick = one_hot(iota((CHUNK, SLOTS), 0) + c * CHUNK == dest_b)
        send_b[pl.ds(c * PLANE, PLANE)] = to_message(dot(pick, res_ext[...]))
        return carry

    lax.fori_loop(0, NZ, pack_res, 0)
    exchange(send_b, recv_b, b_send, b_recv)

    swap_res.wait()
    ones = jnp.ones((16, HALF), BF16)
    row_norm = jnp.zeros((16, SLOTS), F32)
    for f in range(2):
        r = res_full[f].astype(F32)
        row_rhs[:, f * HALF : (f + 1) * HALF] = (-2.0 * r).astype(BF16)
        sq = r * r
        sq_hi = sq.astype(BF16)
        sq_lo = (sq - sq_hi.astype(F32)).astype(BF16)
        row_norm += dot(ones, sq_hi, ((1,), (1,))) + dot(ones, sq_lo, ((1,), (1,)))
    row_norm = row_norm[0:1]

    others(recv_b, b_recv).wait()

    def add_up(c, carry):
        sums, counts = carry
        v, tags = from_message(recv_b[pl.ds(c * PLANE, PLANE)])
        t = dot(eye_t, tags.astype(BF16), ((1,), (1,)))
        word = jnp.where(t[1:2] > 0.0, t[2:3], -1.0).astype(I32)
        word = jnp.where(word >= 0, word & 31, -1)
        pick = iota((32, CHUNK), 0) == word
        sums += dot(one_hot(pick), v.astype(BF16))
        counts += jnp.sum(jnp.where(pick, 1.0, 0.0), axis=1, keepdims=True)
        return sums, counts

    sums, counts = lax.fori_loop(
        0, NZ, add_up, (jnp.zeros((32, HALF), F32), jnp.zeros((32, 1), F32))
    )
    sums_own[0], sums_own[1] = sums[:16], sums[16:]
    swap_sums = pltpu.make_async_remote_copy(
        src_ref=sums_own.at[1 - feat], dst_ref=sums_sib, send_sem=p_send.at[1],
        recv_sem=p_recv.at[1], device_id=sibling, device_id_type=MESH,
    )
    swap_sums.start()
    count = jnp.where(feat == 0, counts[:16], counts[16:])
    mine = jnp.where(feat == 0, sums[:16], sums[16:])
    swap_sums.wait()
    theirs = sums_sib[...]
    total = jnp.concatenate(
        [jnp.where(feat == 0, mine, theirs), jnp.where(feat == 0, theirs, mine)], axis=1
    )
    updated = (total + PRIOR * codebook_ref[...]) / (count + PRIOR)
    updated_ref[...] = updated
    book = updated.astype(BF16)

    place, size = {"x": x, "y": y, "z": z}, {"x": NX, "y": NY, "z": NZ}
    bufs = (book_x, book_y, book_z)
    for p, order in enumerate(ORDERS):
        (c1, c2, c3), (n1, n2, _) = [place[a] for a in order], [size[a] for a in order]
        bufs[p][(c3 * n2 + c2) * n1 + c1] = book[:, p * PART : (p + 1) * PART]

    def neighbour(axis, by):
        d = {"x": 0, "y": 0, "z": 0}
        d[axis] = by
        return (chip(d["z"], d["y"], d["x"]), feat)

    steps = []
    for order in ORDERS:
        todo = []
        for phase, axis in enumerate(order):
            todo += [(phase, axis, k) for k in range(size[axis] // 2)]
        steps.append(todo)

    def block(p, phase, origin, part):
        order = ORDERS[p]
        (c1, c2, c3), (n1, n2, _) = [place[a] for a in order], [size[a] for a in order]
        at, n = (
            ((c3 * n2 + c2) * n1 + origin, 1),
            ((c3 * n2 + origin) * n1, n1),
            (origin * n2 * n1, n1 * n2),
        )[phase]
        if part is None:
            return bufs[p].at[pl.ds(at, n)]
        if n == 1:
            return bufs[p].at[pl.ds(at, 1), :, pl.ds(part * 128, 128)]
        return bufs[p].at[pl.ds(at + part * (n // 2), n // 2)]

    moving = [[], [], []]
    sent = []
    for t in range(len(steps[0])):
        for p in range(3):
            for copy in moving[p]:
                copy.wait_recv()
            phase, axis, k = steps[p][t]
            n, c = size[axis], place[axis]
            last = k == n // 2 - 1
            moving[p] = []
            for d, sign in enumerate((1, -1)):
                ref = block(p, phase, (c + n - sign * k) % n, d if last else None)
                moving[p].append(
                    pltpu.make_async_remote_copy(
                        src_ref=ref, dst_ref=ref, send_sem=g_send.at[p, t, d], recv_sem=g_recv.at[p, t, d],
                        device_id=neighbour(axis, sign % n), device_id_type=MESH,
                    )
                )
                moving[p][-1].start()
            sent += moving[p]
    for p in range(3):
        for copy in moving[p]:
            copy.wait_recv()

    def plane(c, best):
        piece_a = book_x[pl.ds(c * PLANE, PLANE)].reshape(256, PART)
        piece_b = jnp.concatenate(
            [book_y[(i % NX * NZ + c) * NY + i // NX] for i in range(PLANE)], axis=0
        )
        piece_c = jnp.concatenate([book_z[i * NZ + c] for i in range(PLANE)], axis=0)
        piece = jnp.concatenate([piece_a, piece_b, piece_c], axis=1)
        f = piece.astype(F32)
        norm = jnp.sum(f * f, axis=1, keepdims=True)
        dist = dot(piece, row_rhs[...], ((1,), (1,))) + norm
        return jnp.minimum(best, jnp.min(dist.reshape(32, 8, SLOTS), axis=0))

    best = lax.fori_loop(0, NZ, plane, jnp.full((8, SLOTS), 3e38, F32))
    best = (jnp.min(best, axis=0, keepdims=True) + row_norm) / FEATURES
    for c in range(NZ):
        min_send[c] = best[:, c * CHUNK : (c + 1) * CHUNK]

    def give_back(i, carry):
        s = nth(i)
        pltpu.make_async_remote_copy(
            src_ref=min_send.at[s // PLANE], dst_ref=min_recv.at[s], send_sem=e_send, recv_sem=e_recv,
            device_id=behind(s), device_id_type=MESH,
        ).start()
        return carry

    lax.fori_loop(1, CHIPS, give_back, 0)
    min_recv[0] = min_send[0]
    others(min_recv, e_recv).wait()
    pick = one_hot(iota((CHIPS, ROWS), 0) == rel)
    got = jnp.zeros((128, ROWS), F32)
    for piece in split3(min_recv[...].reshape(CHIPS, 128)):
        got += dot(piece, pick, ((0,), (0,)))
    lane = (rel & (PLANE - 1)) * CAP + rank
    near = jnp.sum(jnp.where(iota((128, ROWS), 0) == lane, got, 0.0), axis=0, keepdims=True)
    near_own[...] = near
    swap_near = pltpu.make_async_remote_copy(
        src_ref=near_own, dst_ref=near_sib, send_sem=p_send.at[2],
        recv_sem=p_recv.at[2], device_id=sibling, device_id_type=MESH,
    )
    swap_near.start()
    swap_near.wait()
    nearest_ref[...] = jnp.minimum(near, near_sib[...])

    others(send_a, a_send).wait()
    others(send_b, b_send).wait()
    others(min_recv, e_send).wait()
    for copy in sent:
        copy.wait_send()


def per_device(rows, list_ids, code_ids, list_slot, coarse, codebook):
    vmem = pl.BlockSpec(memory_space=pltpu.VMEM)
    message = pltpu.VMEM((CHIPS, 16, PART), BF16)
    dma = pltpu.SemaphoreType.DMA
    updated, nearest = pl.pallas_call(
        kernel,
        out_shape=(
            jax.ShapeDtypeStruct((16, FEATURES), F32),
            jax.ShapeDtypeStruct((1, ROWS), F32),
        ),
        in_specs=[vmem] * 6,
        out_specs=(vmem, vmem),
        scratch_shapes=[
            pltpu.VMEM((ROWS, 512), BF16),
            message, message, message, message,
            pltpu.VMEM((SLOTS, 512), BF16),
            pltpu.VMEM((2, SLOTS, HALF), BF16),
            pltpu.VMEM((SLOTS, FEATURES), BF16),
            pltpu.VMEM((2, 16, HALF), F32),
            pltpu.VMEM((16, HALF), F32),
            message, message, message,
            pltpu.VMEM((NZ, 1, 128), F32),
            pltpu.VMEM((CHIPS, 1, 128), F32),
            pltpu.VMEM((1, ROWS), F32),
            pltpu.VMEM((1, ROWS), F32),
            dma, dma, dma, dma, dma, dma,
            dma((3, 8, 2)), dma((3, 8, 2)), dma((3,)), dma((3,)),
        ],
        compiler_params=pltpu.CompilerParams(
            collective_id=0, has_side_effects=True, vmem_limit_bytes=48 * 2**20
        ),
    )(
        rows,
        list_ids.reshape(1, ROWS),
        code_ids.reshape(1, ROWS),
        list_slot.reshape(128, 128),
        coarse,
        codebook,
    )
    return updated, nearest.reshape(ROWS)


def solution(mesh):
    placed = (P("rep", "feat"), P("rep"), P("rep"), P(), P("rep", None), P(("rep", "feat"), None))
    return jax.shard_map(
        per_device,
        mesh=mesh,
        in_specs=placed,
        out_specs=(P(("rep", "feat"), None), P("rep")),
        check_vma=False,
    )
```

time: 665 us -> 137 us (0.21)
  waiting for transfers between devices: 494 us -> 0 us
  Pallas kernels: 0 us -> 131 us
  blocking collectives: 80.1 us -> 0 us
  starting transfers between devices: 35.7 us -> 0 us
  between operations: 14.3 us -> 0.66 us
  local copies, waits for them, and re-layouts: 17.9 us -> 5.44 us
  matrix products: 11 us -> 0 us
  other arithmetic: 11 us -> 0 us
    reduce_scatter x1 -> x0, waiting for transfers between devices: 322 us -> none  [per_device(): lax.psum_scatter(partial_sums, ('rep', 'feat'), scatter_dimension=0, tile...]
    pallas_call x0 -> x1, Pallas kernels: none -> 131 us  [per_device(): pl.pallas_call(kernel, out_shape=(jax.ShapeDtypeStruct((16, FEATURES), F3...]
    all_gather x1 -> x0, waiting for transfers between devices: 120 us -> none  [per_device(): piece = lax.all_gather(book_piece, ('rep', 'feat'), axis=0, tiled=True)]
    unnamed x1 -> x0, blocking collectives: 75.4 us -> none
    all_to_all x3 -> x0, waiting for transfers between devices: 51.9 us -> none  [the longest x1 36.8 us: per_device(): lax.all_to_all(packed, 'rep', split_axis=0, concat_axis=0, tiled=True)]
    all_to_all x3 -> x0, starting transfers between devices: 35.4 us -> none  [the longest x1 16.3 us: per_device(): lax.all_to_all(packed_meta, 'rep', split_axis=0, concat_axis=0, tiled=True)]
    dot_general x2 -> x0, matrix products: 11 us -> none  [the longest x1 6.85 us: per_device(): lax.dot_general(code_hits, res_b, (((0,), (0,)), ((), ())), preferred_ele...]
    gather x3 -> x0, local copies, waits for them, and re-layouts: 7.84 us -> none  [the longest x1 3.52 us: per_device(): slot = jnp.take(list_slot, list_ids)]
  transfers between devices with their start and end apart: 5 -> 0, of which waited for: 5 -> 0; matrix products, arithmetic and copies ran while one was open for 1% -> 0% of each run, Pallas kernels for 0% -> 0%
where the time goes in v1:
time: 137 us
  Pallas kernels  131 us (96%)
  local copies, waits for them, and re-layouts  5.44 us (4%)
    pallas_call x1, Pallas kernels, per_device(): pl.pallas_call(kernel, out_shape=(jax.ShapeDtypeStruct((16, FEATURES), F3...  131 us
    unnamed x14, local copies, waits for them, and re-layouts  5.44 us

profile of v1, /device:TPU:1, one launch (start us, length us, event | category | flops | bytes accessed | tf_op | source)
XLA Modules:
  0.0 137.2 jit_solution(3328721885246313893)
XLA Ops:
  0.6 0.0 copy-start.5
  0.6 0.0 copy-start.4
  0.7 0.7 copy-done.5
  1.3 0.0 copy-done.4
  1.3 0.0 copy-start
  1.3 1.0 copy-done
  2.3 0.0 copy-start.1
  2.3 0.9 copy-done.1
  3.3 0.0 copy-start.2
  3.3 0.8 copy-done.2
  4.1 0.0 copy-start.3
  4.1 0.8 copy-done.3
  4.9 131.1 %shard_map.77 = (f32[16,768]{1,0:T(8,128)S(1)}, f32[1,512]{1,0:T(1,128)S(1)}) custom-call(bf16[512,384]{1,0:T(8,128)(2,1)S(1)} %copy-done, s32[1,512]{1,0:T(1,128)S(1)} %bitcast.5, s32[1,512]{1,0:T(1,128)S(1)} %bitcast.6, s32[128,128]{1,0:T(8,128)S(1)} %bitcast.4, bf16[128,768]{1,0:T(8,128)(2,1)S(1)} %copy-done.1, f32[16,768]{1,0:T(8,128)S(1)} %copy-done.3), custom_call_target="tpu_custom_call" | custom-call | tf_op jit(solution)/shard_map/pallas_call | solution.py:353
  136.0 0.6 copy.10
  136.6 0.6 copy.11
Async XLA Ops:
  0.6 0.7 copy-start.5
  0.6 0.7 copy-start.4
  1.3 1.0 copy-start
  2.3 0.9 copy-start.1
  3.3 0.8 copy-start.2
  4.1 0.8 copy-start.3

commit v2 on v0

v2 whole, which is shorter than its diff:
```python
import jax
import jax.numpy as jnp
from jax import lax
from jax.experimental import pallas as pl
from jax.experimental.pallas import tpu as pltpu
from jax.sharding import PartitionSpec as P

NZ, NY, NX = 8, 4, 4
PLANE = NY * NX
CHIPS = NZ * PLANE
FEATURES = 768
HALF = FEATURES // 2
PART = FEATURES // 3
ROWS = 512
CAP = 8
CHUNK = PLANE * CAP
SLOTS = CHIPS * CAP
PRIOR = 8.0
MESH = pl.DeviceIdType.MESH
F32, BF16, I32 = jnp.float32, jnp.bfloat16, jnp.int32
NEAR_FIRST = (0, 1, 7, 2, 6, 3, 5, 4)


def iota(shape, axis):
    return lax.broadcasted_iota(I32, shape, axis)


def one_hot(mask):
    return jnp.where(mask, 1.0, 0.0).astype(BF16)


def dot(a, b, over=((1,), (0,))):
    return lax.dot_general(a, b, (over, ((), ())), preferred_element_type=F32)


def to_messages(v):
    v = v.reshape(PLANE, CAP, HALF)
    return jnp.concatenate([v[:, :, i * 128 : (i + 1) * 128] for i in range(3)], axis=1).astype(BF16)


def from_messages(m):
    m = m.astype(F32)
    return jnp.concatenate(
        [m[:, i * CAP : (i + 1) * CAP, :].reshape(CHUNK, 128) for i in range(3)], axis=1
    )


def kernel(
    rows_hbm, lid_hbm, code_hbm, table_hbm, coarse_hbm, codebook_hbm,
    updated_ref, nearest_ref,
    rows_ref, lid_ref, code_ref, table_ref, coarse_ref, codebook_ref,
    send_a, mid_a, recv_a, send_b, mid_b, recv_b,
    tag_send, tag_mid, tag_recv, pick_b, res_full, row_rhs,
    sums_own, sums_sib, book_a, book_c, book_d, near_own, near_sib,
    load_sem, z_send, z_recv, p_send, p_recv, tag_sem, swap_send, swap_recv,
    t0_send, t0_recv, t1_send, t1_recv, ring_send, ring_recv,
):
    rep, feat = lax.axis_index("rep"), lax.axis_index("feat")
    z, y, x = rep >> 4, (rep >> 2) & 3, rep & 3

    def chip(dz, dy, dx):
        at = (((z + dz) & (NZ - 1)) << 4) | (((y + dy) & 3) << 2) | ((x + dx) & 3)
        return (at, feat)

    def in_plane(p, sign=1):
        return chip(0, sign * (p >> 2), sign * (p & 3))

    sibling = (rep, 1 - feat)

    def remote(src, dst, send_sem, recv_sem, to):
        return pltpu.make_async_remote_copy(
            src_ref=src, dst_ref=dst, send_sem=send_sem, recv_sem=recv_sem,
            device_id=to, device_id_type=MESH,
        )

    def wait_bytes(ref, sem):
        pltpu.make_async_copy(ref, ref, sem).wait()

    loads = [
        pltpu.make_async_copy(src, dst, load_sem.at[i])
        for i, (src, dst) in enumerate(
            (
                (lid_hbm, lid_ref),
                (table_hbm, table_ref),
                (code_hbm, code_ref),
                (rows_hbm, rows_ref),
                (coarse_hbm.at[:, pl.ds(pl.multiple_of(feat * HALF, 128), HALF)], coarse_ref),
                (codebook_hbm, codebook_ref),
            )
        )
    ]
    for load in loads:
        load.start()
    barrier = pltpu.get_barrier_semaphore()
    for p in range(1, PLANE):
        pl.semaphore_signal(barrier, inc=1, device_id=in_plane(p), device_id_type=MESH)
    for dz in range(1, NZ):
        pl.semaphore_signal(barrier, inc=1, device_id=chip(dz, 0, 0), device_id_type=MESH)
    pl.semaphore_signal(barrier, inc=1, device_id=sibling, device_id_type=MESH)

    for load in loads[:3]:
        load.wait()
    lid, code, table = lid_ref[...], code_ref[...], table_ref[...]
    high = one_hot(iota((128, ROWS), 0) == (lid >> 7))
    low = iota((128, ROWS), 0) == (lid & 127)

    def look_up(t):
        got = dot(t.astype(F32).astype(BF16), high, ((0,), (0,)))
        return jnp.sum(jnp.where(low, got, 0.0), axis=0, keepdims=True)

    owner, local = look_up(table >> 7), look_up(table & 127)

    def offset(chip_id):
        return (
            (((chip_id >> 4) - z) & (NZ - 1)) * PLANE
            + (((chip_id >> 2) - y) & (NY - 1)) * NX
            + ((chip_id - x) & (NX - 1))
        )

    def lines(values, width):
        line, out = iota((16, width), 0), jnp.zeros((16, width), F32)
        for i, v in enumerate(values):
            out = jnp.where(line == i, v, out)
        return out.astype(BF16)

    owner_col = dot(lines([owner], ROWS), lines([1.0], ROWS), ((0,), (0,)))
    same = (owner_col == owner) & (iota((ROWS, ROWS), 0) < iota((ROWS, ROWS), 1))
    rank = jnp.sum(jnp.where(same, 1.0, 0.0), axis=0, keepdims=True).astype(I32)
    dest = offset(owner.astype(I32)) * CAP + rank
    tags = lines([local, (code >> 6).astype(F32), (code & 63).astype(F32), 1.0], ROWS)
    loads[3].wait()

    def pack_rows(c, carry):
        pick = one_hot(iota((CHUNK, ROWS), 0) + c * CHUNK == dest)
        send_a[c] = to_messages(dot(pick, rows_ref[...]))
        t = dot(tags, pick, ((1,), (1,)))
        tag_send[0, c] = t[0:1] * 4096.0 + t[1:2] * 64.0 + t[2:3] + t[3:4]
        return carry

    lax.fori_loop(0, NZ, pack_rows, 0)
    loads[4].wait()
    loads[5].wait()
    pl.semaphore_wait(barrier, PLANE + NZ - 1)

    def tags_along_z(n, sign):
        for dz in range(1, NZ):
            remote(tag_send.at[n, dz], tag_mid.at[n, dz], tag_sem.at[n, 0], tag_sem.at[n, 1],
                   chip(sign * dz, 0, 0)).start()
        tag_mid[n, 0] = tag_send[n, 0]

    def tags_in_plane(n, sign):
        wait_bytes(tag_mid.at[n, pl.ds(1, NZ - 1)], tag_sem.at[n, 1])
        for p in range(1, PLANE):
            remote(tag_mid.at[n], tag_recv.at[n, p], tag_sem.at[n, 2], tag_sem.at[n, 3],
                   in_plane(p, sign)).start()
        tag_recv[n, 0] = tag_mid[n]

    def tags_got(n):
        wait_bytes(tag_recv.at[n, pl.ds(1, PLANE - 1)], tag_sem.at[n, 3])
        lane = iota((NZ, 128), 1) >> 3
        out = jnp.zeros((NZ, 128), F32)
        for p in range(PLANE):
            out = jnp.where(lane == p, tag_recv[n, p].reshape(NZ, 128), out)
        return out

    def tags_sent(n):
        wait_bytes(tag_send.at[n, pl.ds(1, NZ - 1)], tag_sem.at[n, 0])
        wait_bytes(tag_recv.at[n, pl.ds(1, PLANE - 1)], tag_sem.at[n, 2])

    def in_a_row(t):
        return jnp.concatenate([t[c : c + 1] for c in range(NZ)], axis=1)

    def along_z(n, src, mid, dz):
        remote(src.at[dz], mid.at[dz], z_send.at[n], z_recv.at[n, dz], chip(dz, 0, 0)).start()

    def forward(n, src, mid, dst, dz):
        held = mid
        if dz == 0:
            held = src
        else:
            wait_bytes(mid.at[dz], z_recv.at[n, dz])

        def start(p, carry):
            remote(held.at[dz, p], dst.at[dz, p], p_send.at[n], p_recv.at[n, dz], in_plane(p)).start()
            return carry

        lax.fori_loop(1, PLANE, start, 0)
        dst[dz, 0] = held[dz, 0]

    def arrived(n, dst, dz):
        wait_bytes(dst.at[dz, pl.ds(1, PLANE - 1)], p_recv.at[n, dz])
        return from_messages(dst[dz])

    def all_sent(n, src, dst):
        wait_bytes(src.at[pl.ds(1, NZ - 1)], z_send.at[n])
        for dz in range(NZ):
            wait_bytes(dst.at[dz, pl.ds(1, PLANE - 1)], p_send.at[n])

    tags_along_z(0, 1)
    for dz in NEAR_FIRST[1:]:
        along_z(0, send_a, mid_a, dz)
    forward(0, send_a, mid_a, recv_a, 0)
    tags_in_plane(0, 1)
    forward(0, send_a, mid_a, recv_a, 1)
    forward(0, send_a, mid_a, recv_a, 7)

    got = in_a_row(tags_got(0)).astype(I32) - 1
    local_b = got >> 12
    code_b = jnp.where(got >= 0, got & 4095, -1)
    half_b = ((z - (iota((1, SLOTS), 1) >> 7)) & (NZ - 1)) >> 2
    key = jnp.where(got >= 0, (code_b >> 4) * 2 + half_b, -1)
    key_f = key.astype(F32)
    key_lines = lines([(key >> 4).astype(F32), (key & 15).astype(F32)], SLOTS)
    weights = lines([16.0, 1.0], SLOTS)
    rank_b = jnp.zeros((1, SLOTS), F32)
    for c in range(NZ):
        key_col = dot(key_lines[:, c * CHUNK : (c + 1) * CHUNK], weights, ((0,), (0,)))
        before = iota((CHUNK, SLOTS), 0) + c * CHUNK < iota((CHUNK, SLOTS), 1)
        hit = jnp.where((key_col == key_f) & before, 1.0, 0.0)
        rank_b += jnp.sum(hit, axis=0, keepdims=True)
    dest_b = offset(code_b >> 5) * CAP + ((code_b >> 4) & 1) * 4 + half_b * 2 + rank_b.astype(I32)
    dest_b = jnp.where(got >= 0, dest_b, -1)
    tags_b = lines([(code_b & 31).astype(F32), 1.0], SLOTS)

    def plan(c, carry):
        pick = one_hot(iota((CHUNK, SLOTS), 0) + c * CHUNK == dest_b)
        pick_b[pl.ds(c * CHUNK, CHUNK), :] = pick
        t = dot(tags_b, pick, ((1,), (1,)))
        tag_send[1, c] = t[0:1] + t[1:2]
        return carry

    lax.fori_loop(0, NZ, plan, 0)
    tags_along_z(1, 1)

    def residual(dz):
        v = arrived(0, recv_a, dz)
        pick = one_hot(iota((128, CHUNK), 0) == local_b[:, dz * CHUNK : (dz + 1) * CHUNK])
        res = (v - dot(pick, coarse_ref[...], ((0,), (0,)))).astype(BF16)
        res_full[feat, pl.ds(dz * CHUNK, CHUNK), :] = res

    forward(0, send_a, mid_a, recv_a, 2)
    forward(0, send_a, mid_a, recv_a, 6)
    residual(0)
    residual(1)
    residual(7)
    tags_in_plane(1, 1)
    forward(0, send_a, mid_a, recv_a, 3)
    forward(0, send_a, mid_a, recv_a, 5)
    residual(2)
    residual(6)
    forward(0, send_a, mid_a, recv_a, 4)
    residual(3)
    residual(5)
    residual(4)

    for dz in NEAR_FIRST[1:] + (0,):
        pick = pick_b[dz * CHUNK : (dz + 1) * CHUNK, :]
        send_b[dz] = to_messages(dot(pick, res_full[feat]))
        if dz:
            along_z(1, send_b, mid_b, dz)
    swap_res = remote(res_full.at[feat], res_full.at[feat], swap_send.at[0], swap_recv.at[0], sibling)
    swap_res.start()
    forward(1, send_b, mid_b, recv_b, 0)
    word = in_a_row(tags_got(1)).astype(I32) - 1
    forward(1, send_b, mid_b, recv_b, 1)
    forward(1, send_b, mid_b, recv_b, 7)

    swap_res.wait()
    ones = jnp.ones((16, HALF), BF16)
    row_norm = jnp.zeros((16, SLOTS), F32)
    for f in range(2):
        r = res_full[f].astype(F32)
        row_rhs[:, f * HALF : (f + 1) * HALF] = (-2.0 * r).astype(BF16)
        sq = r * r
        sq_hi = sq.astype(BF16)
        sq_lo = (sq - sq_hi.astype(F32)).astype(BF16)
        row_norm += dot(ones, sq_hi, ((1,), (1,))) + dot(ones, sq_lo, ((1,), (1,)))
    row_norm = row_norm[0:1]

    sums, counts = jnp.zeros((32, HALF), F32), jnp.zeros((32, 1), F32)

    def add_up(dz, sums, counts):
        v = arrived(1, recv_b, dz).astype(BF16)
        pick = iota((32, CHUNK), 0) == word[:, dz * CHUNK : (dz + 1) * CHUNK]
        counts += jnp.sum(jnp.where(pick, 1.0, 0.0), axis=1, keepdims=True)
        return sums + dot(one_hot(pick), v), counts

    forward(1, send_b, mid_b, recv_b, 2)
    forward(1, send_b, mid_b, recv_b, 6)
    for dz in (0, 1, 7):
        sums, counts = add_up(dz, sums, counts)
    forward(1, send_b, mid_b, recv_b, 3)
    forward(1, send_b, mid_b, recv_b, 5)
    for dz in (2, 6):
        sums, counts = add_up(dz, sums, counts)
    forward(1, send_b, mid_b, recv_b, 4)
    for dz in (3, 5, 4):
        sums, counts = add_up(dz, sums, counts)
    sums_own[0], sums_own[1] = sums[:16], sums[16:]
    swap_sums = remote(sums_own.at[1 - feat], sums_sib, swap_send.at[1], swap_recv.at[1], sibling)
    swap_sums.start()
    count = jnp.where(feat == 0, counts[:16], counts[16:])
    mine = jnp.where(feat == 0, sums[:16], sums[16:])
    swap_sums.wait()
    theirs = sums_sib[...]
    total = jnp.concatenate(
        [jnp.where(feat == 0, mine, theirs), jnp.where(feat == 0, theirs, mine)], axis=1
    )
    updated = (total + PRIOR * codebook_ref[...]) / (count + PRIOR)
    updated_ref[...] = updated
    book = updated.astype(BF16)

    at_a, at_c, at_d = (z * NY + y) * NX + x, (y * NX + x) * NZ + z, (x * NY + y) * NZ + z
    book_a[at_a] = book[:, :PART]
    book_c[at_c] = book[:, PART : 2 * PART]
    book_d[at_d] = book[:, 2 * PART :]
    for dz in range(1, NZ):
        for i, (buf, at) in enumerate(((book_c, at_c), (book_d, at_d))):
            remote(buf.at[at], buf.at[at], t0_send.at[i], t0_recv.at[i], chip(dz, 0, 0)).start()
    for p in range(1, PLANE):
        remote(book_a.at[at_a], book_a.at[at_a], t0_send.at[2], t0_recv.at[2], in_plane(p)).start()

    sent = []

    def ring(n, buf, place, size, block, step, k):
        half = block // 2
        copies = []
        for d, sign in enumerate((1, -1)):
            at = ((place - sign * k) & (size - 1)) * block
            ref = buf.at[pl.ds(at, block)]
            if k == size // 2 - 1:
                ref = buf.at[pl.ds(at + d * half, half)]
            to = chip(*(sign * s for s in step))
            copies.append(remote(ref, ref, ring_send.at[n, k, d], ring_recv.at[n, k, d], to))
        for copy in copies:
            copy.start()
        sent.extend(copies)
        return copies

    def came(copies):
        for copy in copies:
            copy.wait_recv()

    def ring_a(k):
        return ring(0, book_a, z, NZ, PLANE, (1, 0, 0), k)

    def ring_c(k):
        return ring(1, book_c, y, NY, NX * NZ, (0, 1, 0), k)

    def ring_d(k):
        return ring(2, book_d, x, NX, NY * NZ, (0, 0, 1), k)

    wait_bytes(book_c.at[pl.ds(0, NZ - 1)], t0_recv.at[0])
    wait_bytes(book_d.at[pl.ds(0, NZ - 1)], t0_recv.at[1])
    line_c = book_c.at[pl.ds((y * NX + x) * NZ, NZ)]
    line_d = book_d.at[pl.ds((x * NY + y) * NZ, NZ)]
    for i in range(1, NX):
        remote(line_c, line_c, t1_send.at[0], t1_recv.at[0], chip(0, 0, i)).start()
        remote(line_d, line_d, t1_send.at[1], t1_recv.at[1], chip(0, i, 0)).start()
    wait_bytes(book_a.at[pl.ds(0, PLANE - 1)], t0_recv.at[2])
    a0 = ring_a(0)
    wait_bytes(book_c.at[pl.ds(0, 3 * NZ)], t1_recv.at[0])
    c0 = ring_c(0)
    wait_bytes(book_d.at[pl.ds(0, 3 * NZ)], t1_recv.at[1])
    d0 = ring_d(0)
    came(a0)
    a1 = ring_a(1)
    came(c0)
    c1 = ring_c(1)
    came(d0)
    d1 = ring_d(1)
    came(a1)
    a2 = ring_a(2)
    came(a2)
    a3 = ring_a(3)
    came(c1)
    came(d1)
    came(a3)

    def book_sent():
        for i, (buf, n) in enumerate(((book_c, NZ - 1), (book_d, NZ - 1), (book_a, PLANE - 1))):
            wait_bytes(buf.at[pl.ds(0, n)], t0_send.at[i])
        for i, buf in enumerate((book_c, book_d)):
            wait_bytes(buf.at[pl.ds(0, 3 * NZ)], t1_send.at[i])
        for copy in sent:
            copy.wait_send()


    def plane(c, best):
        piece_a = book_a[pl.ds(c * PLANE, PLANE)].reshape(256, PART)
        piece_c = jnp.concatenate([book_c[i * NZ + c] for i in range(PLANE)], axis=0)
        piece_d = jnp.concatenate(
            [book_d[(i % NX * NY + i // NX) * NZ + c] for i in range(PLANE)], axis=0
        )
        piece = jnp.concatenate([piece_a, piece_c, piece_d], axis=1)
        f = piece.astype(F32)
        norm = jnp.sum(f * f, axis=1, keepdims=True)
        dist = dot(piece, row_rhs[...], ((1,), (1,))) + norm
        return jnp.minimum(best, jnp.min(dist.reshape(32, 8, SLOTS), axis=0))

    best = lax.fori_loop(0, NZ, plane, jnp.full((8, SLOTS), 3e38, F32))
    best = (jnp.min(best, axis=0, keepdims=True) + row_norm) / FEATURES
    for c in range(NZ):
        tag_send[2, c] = best[:, c * CHUNK : (c + 1) * CHUNK]

    tags_along_z(2, -1)
    tags_in_plane(2, -1)
    back = tags_got(2)
    parts = []
    for _ in range(3):
        parts.append(back.astype(BF16).astype(F32))
        back = back - parts[-1]
    lane = one_hot(iota((128, ROWS), 0) == (dest & 127))
    near = dot(jnp.concatenate(parts, axis=0).astype(BF16), lane)
    near = near[:8] + near[8:16] + near[16:]
    near = jnp.sum(jnp.where(iota((NZ, ROWS), 0) == (dest >> 7), near, 0.0), axis=0, keepdims=True)
    near_own[...] = near
    swap_near = remote(near_own, near_sib, swap_send.at[2], swap_recv.at[2], sibling)
    swap_near.start()

    for n in range(3):
        tags_sent(n)
    all_sent(0, send_a, recv_a)
    all_sent(1, send_b, recv_b)
    book_sent()
    swap_near.wait()
    nearest_ref[...] = jnp.minimum(near, near_sib[...])


def per_device(rows, list_ids, code_ids, list_slot, coarse, codebook):
    vmem, hbm = pl.BlockSpec(memory_space=pltpu.VMEM), pl.BlockSpec(memory_space=pl.ANY)
    messages = pltpu.VMEM((NZ, PLANE, 24, 128), BF16)
    blocks = pltpu.VMEM((CHIPS, 16, PART), BF16)
    dma = pltpu.SemaphoreType.DMA
    updated, nearest = pl.pallas_call(
        kernel,
        out_shape=(
            jax.ShapeDtypeStruct((16, FEATURES), F32),
            jax.ShapeDtypeStruct((1, ROWS), F32),
        ),
        in_specs=[hbm] * 6,
        out_specs=(vmem, vmem),
        scratch_shapes=[
            pltpu.VMEM((ROWS, HALF), BF16),
            pltpu.VMEM((1, ROWS), I32),
            pltpu.VMEM((1, ROWS), I32),
            pltpu.VMEM((128, 128), I32),
            pltpu.VMEM((128, HALF), BF16),
            pltpu.VMEM((16, FEATURES), F32),
            messages, messages, messages, messages, messages, messages,
            pltpu.VMEM((3, NZ, 1, 128), F32),
            pltpu.VMEM((3, NZ, 1, 128), F32),
            pltpu.VMEM((3, PLANE, NZ, 1, 128), F32),
            pltpu.VMEM((SLOTS, SLOTS), BF16),
            pltpu.VMEM((2, SLOTS, HALF), BF16),
            pltpu.VMEM((SLOTS, FEATURES), BF16),
            pltpu.VMEM((2, 16, HALF), F32),
            pltpu.VMEM((16, HALF), F32),
            blocks, blocks, blocks,
            pltpu.VMEM((1, ROWS), F32),
            pltpu.VMEM((1, ROWS), F32),
            dma((6,)), dma((2,)), dma((2, NZ)), dma((2,)), dma((2, NZ)), dma((3, 4)), dma((3,)), dma((3,)),
            dma((3,)), dma((3,)), dma((2,)), dma((2,)), dma((3, 4, 2)), dma((3, 4, 2)),
        ],
        compiler_params=pltpu.CompilerParams(
            collective_id=0, has_side_effects=True, vmem_limit_bytes=63 * 2**20
        ),
    )(
        rows,
        list_ids.reshape(1, ROWS),
        code_ids.reshape(1, ROWS),
        list_slot.reshape(128, 128),
        coarse,
        codebook,
    )
    return updated, nearest.reshape(ROWS)


def solution(mesh):
    placed = (P("rep", "feat"), P("rep"), P("rep"), P(), P("rep", None), P(("rep", "feat"), None))
    return jax.shard_map(
        per_device,
        mesh=mesh,
        in_specs=placed,
        out_specs=(P(("rep", "feat"), None), P("rep")),
        check_vma=False,
    )
```

time: 665 us -> 111 us (0.17)
  waiting for transfers between devices: 494 us -> 0 us
  Pallas kernels: 0 us -> 108 us
  blocking collectives: 80.1 us -> 0 us
  starting transfers between devices: 35.7 us -> 0 us
  local copies, waits for them, and re-layouts: 17.9 us -> 2.01 us
  between operations: 14.3 us -> 0.65 us
  matrix products: 11 us -> 0 us
  other arithmetic: 11 us -> 0 us
    reduce_scatter x1 -> x0, waiting for transfers between devices: 322 us -> none  [per_device(): lax.psum_scatter(partial_sums, ('rep', 'feat'), scatter_dimension=0, tile...]
    all_gather x1 -> x0, waiting for transfers between devices: 120 us -> none  [per_device(): piece = lax.all_gather(book_piece, ('rep', 'feat'), axis=0, tiled=True)]
    pallas_call x0 -> x1, Pallas kernels: none -> 108 us  [per_device(): pl.pallas_call(kernel, out_shape=(jax.ShapeDtypeStruct((16, FEATURES), F3...]
    unnamed x1 -> x0, blocking collectives: 75.4 us -> none
    all_to_all x3 -> x0, waiting for transfers between devices: 51.9 us -> none  [the longest x1 36.8 us: per_device(): lax.all_to_all(packed, 'rep', split_axis=0, concat_axis=0, tiled=True)]
    all_to_all x3 -> x0, starting transfers between devices: 35.4 us -> none  [the longest x1 16.3 us: per_device(): lax.all_to_all(packed_meta, 'rep', split_axis=0, concat_axis=0, tiled=True)]
    dot_general x2 -> x0, matrix products: 11 us -> none  [the longest x1 6.85 us: per_device(): lax.dot_general(code_hits, res_b, (((0,), (0,)), ((), ())), preferred_ele...]
    gather x3 -> x0, local copies, waits for them, and re-layouts: 7.84 us -> none  [the longest x1 3.52 us: per_device(): slot = jnp.take(list_slot, list_ids)]
  transfers between devices with their start and end apart: 5 -> 0, of which waited for: 5 -> 0; matrix products, arithmetic and copies ran while one was open for 1% -> 0% of each run, Pallas kernels for 0% -> 0%
where the time goes in v2:
time: 111 us
  Pallas kernels  108 us (97%)
  local copies, waits for them, and re-layouts  2.01 us (2%)
    pallas_call x1, Pallas kernels, per_device(): pl.pallas_call(kernel, out_shape=(jax.ShapeDtypeStruct((16, FEATURES), F3...  108 us

profile of v2, /device:TPU:1, one launch (start us, length us, event | category | flops | bytes accessed | tf_op | source)
XLA Modules:
  0.0 111.1 jit_solution(7515136191493998128)
XLA Ops:
  0.6 108.5 %shard_map.77 = (f32[16,768]{1,0:T(8,128)}, f32[1,512]{1,0:T(1,128)}) custom-call(bf16[512,384]{1,0:T(8,128)(2,1)} %rows_hbm.1, s32[1,512]{1,0:T(1,128)} %bitcast.5, s32[1,512]{1,0:T(1,128)} %bitcast.6, s32[128,128]{1,0:T(8,128)} %bitcast.4, bf16[128,768]{1,0:T(8,128)(2,1)} %coarse_hbm.1, f32[16,768]{1,0:T(8,128)} %codebook_hbm.1), custom_call_target="tpu_custom_call" | custom-call | tf_op jit(solution)/shard_map/pallas_call | solution.py:435
  109.1 0.0 copy-start
  109.1 1.4 %copy.10 = f32[16,768]{1,0:T(8,128)} copy(f32[16,768]{1,0:T(8,128)} %get-tuple-element.8) | data formatting | bytes 98304
  110.5 0.0 copy-done
  110.5 0.6 copy.11
Async XLA Ops:
  109.1 1.4 %copy-start = (f32[1,512]{1,0:T(1,128)S(1)}, f32[1,512]{1,0:T(1,128)}, u32[]{:S(2)}) copy-start(f32[1,512]{1,0:T(1,128)} %get-tuple-element.5) | copy-start | bytes 6148

commit v3 on v2

v3 whole, which is shorter than its diff:
```python
import jax
import jax.numpy as jnp
from jax import lax
from jax.experimental import pallas as pl
from jax.experimental.pallas import tpu as pltpu
from jax.sharding import PartitionSpec as P

NZ, NY, NX = 8, 4, 4
PLANE = NY * NX
CHIPS = NZ * PLANE
FEATURES = 768
HALF = FEATURES // 2
PART = FEATURES // 3
ROWS = 512
CAP = 8
CHUNK = PLANE * CAP
SLOTS = CHIPS * CAP
PRIOR = 8.0
MESH = pl.DeviceIdType.MESH
F32, BF16, I32 = jnp.float32, jnp.bfloat16, jnp.int32
SLAB = 4 * NZ
PARTS = 3


def iota(shape, axis):
    return lax.broadcasted_iota(I32, shape, axis)


def one_hot(mask):
    return jnp.where(mask, 1.0, 0.0).astype(BF16)


def dot(a, b, over=((1,), (0,))):
    return lax.dot_general(a, b, (over, ((), ())), preferred_element_type=F32)


def kernel(
    rows_hbm, lid_hbm, code_hbm, table_hbm, coarse_hbm, codebook_hbm,
    updated_ref, nearest_ref,
    rows_ref, lid_ref, code_ref, table_ref, coarse_ref, codebook_ref,
    send_a, mid_a, recv_a, send_b, mid_b, recv_b,
    tag_send, tag_mid, tag_recv, pick_b, base_ref, res_full, row_rhs, acc_ref,
    sums_own, sums_sib, books, near_own, near_sib,
    load_sem, z_send, z_recv, p_send, p_recv, tag_sem, swap_send, swap_recv, g_send, g_recv, r_send, r_recv,
):
    rep, feat = lax.axis_index("rep"), lax.axis_index("feat")
    z, y, x = rep >> 4, (rep >> 2) & 3, rep & 3

    def chip(dz, dy, dx):
        at = (((z + dz) & (NZ - 1)) << 4) | (((y + dy) & 3) << 2) | ((x + dx) & 3)
        return (at, feat)

    def in_plane(p, sign=1):
        return chip(0, sign * (p >> 2), sign * (p & 3))

    sibling = (rep, 1 - feat)

    def remote(src, dst, send_sem, recv_sem, to):
        return pltpu.make_async_remote_copy(
            src_ref=src, dst_ref=dst, send_sem=send_sem, recv_sem=recv_sem,
            device_id=to, device_id_type=MESH,
        )

    def wait_bytes(ref, sem):
        pltpu.make_async_copy(ref, ref, sem).wait()

    loads = [
        pltpu.make_async_copy(src, dst, load_sem.at[i])
        for i, (src, dst) in enumerate(
            (
                (lid_hbm, lid_ref),
                (table_hbm, table_ref),
                (code_hbm, code_ref),
                (rows_hbm, rows_ref),
                (coarse_hbm.at[:, pl.ds(pl.multiple_of(feat * HALF, 128), HALF)], coarse_ref),
                (codebook_hbm, codebook_ref),
            )
        )
    ]
    for load in loads:
        load.start()
    barrier = pltpu.get_barrier_semaphore()
    for p in range(1, PLANE):
        pl.semaphore_signal(barrier, inc=1, device_id=in_plane(p), device_id_type=MESH)
    for dz in range(1, NZ):
        pl.semaphore_signal(barrier, inc=1, device_id=chip(dz, 0, 0), device_id_type=MESH)
    pl.semaphore_signal(barrier, inc=1, device_id=sibling, device_id_type=MESH)

    for load in loads[:3]:
        load.wait()
    lid, code, table = lid_ref[...], code_ref[...], table_ref[...]
    high = one_hot(iota((128, ROWS), 0) == (lid >> 7))
    low = iota((128, ROWS), 0) == (lid & 127)

    def look_up(t):
        got = dot(t.astype(F32).astype(BF16), high, ((0,), (0,)))
        return jnp.sum(jnp.where(low, got, 0.0), axis=0, keepdims=True)

    owner, local = look_up(table >> 7), look_up(table & 127)

    def offset(chip_id):
        return (
            (((chip_id >> 4) - z) & (NZ - 1)) * PLANE
            + (((chip_id >> 2) - y) & (NY - 1)) * NX
            + ((chip_id - x) & (NX - 1))
        )

    def lines(values, width):
        line, out = iota((16, width), 0), jnp.zeros((16, width), F32)
        for i, v in enumerate(values):
            out = jnp.where(line == i, v, out)
        return out.astype(BF16)

    owner_col = dot(lines([owner], ROWS), lines([1.0], ROWS), ((0,), (0,)))
    same = (owner_col == owner) & (iota((ROWS, ROWS), 0) < iota((ROWS, ROWS), 1))
    rank = jnp.sum(jnp.where(same, 1.0, 0.0), axis=0, keepdims=True).astype(I32)
    dest = offset(owner.astype(I32)) * CAP + rank
    tags = lines([local, (code >> 6).astype(F32), (code & 63).astype(F32), 1.0], ROWS)
    loads[3].wait()

    def pack_rows(c, carry):
        pick = one_hot(iota((CHUNK, ROWS), 0) + c * CHUNK == dest)
        out = dot(pick, rows_ref[...])
        for i in range(PARTS):
            send_a[i, c] = out[:, i * 128 : (i + 1) * 128].reshape(PLANE, CAP, 128).astype(BF16)
        t = dot(tags, pick, ((1,), (1,)))
        tag_send[0, c] = t[0:1] * 4096.0 + t[1:2] * 64.0 + t[2:3] + t[3:4]
        return carry

    lax.fori_loop(0, NZ, pack_rows, 0)
    loads[4].wait()
    loads[5].wait()
    pl.semaphore_wait(barrier, PLANE + NZ - 1)

    def tags_along_z(n, sign):
        for dz in range(1, NZ):
            remote(tag_send.at[n, dz], tag_mid.at[n, dz], tag_sem.at[n, 0], tag_sem.at[n, 1],
                   chip(sign * dz, 0, 0)).start()
        tag_mid[n, 0] = tag_send[n, 0]

    def tags_in_plane(n, sign):
        wait_bytes(tag_mid.at[n, pl.ds(1, NZ - 1)], tag_sem.at[n, 1])
        for p in range(1, PLANE):
            remote(tag_mid.at[n], tag_recv.at[n, p], tag_sem.at[n, 2], tag_sem.at[n, 3],
                   in_plane(p, sign)).start()
        tag_recv[n, 0] = tag_mid[n]

    def tags_got(n):
        wait_bytes(tag_recv.at[n, pl.ds(1, PLANE - 1)], tag_sem.at[n, 3])
        lane = iota((NZ, 128), 1) >> 3
        out = jnp.zeros((NZ, 128), F32)
        for p in range(PLANE):
            out = jnp.where(lane == p, tag_recv[n, p].reshape(NZ, 128), out)
        return out

    def tags_sent(n):
        wait_bytes(tag_send.at[n, pl.ds(1, NZ - 1)], tag_sem.at[n, 0])
        wait_bytes(tag_recv.at[n, pl.ds(1, PLANE - 1)], tag_sem.at[n, 2])

    def in_a_row(t):
        return jnp.concatenate([t[c : c + 1] for c in range(NZ)], axis=1)

    def along_z(n, src, mid, i):
        for dz in (4, 3, 5, 2, 6, 1, 7):
            remote(src.at[i, dz], mid.at[i, dz], z_send.at[n], z_recv.at[n, i], chip(dz, 0, 0)).start()
        mid[i, 0] = src[i, 0]

    def forward(n, mid, dst, i):
        wait_bytes(mid.at[i, pl.ds(1, NZ - 1)], z_recv.at[n, i])
        for p in range(1, PLANE):
            remote(mid.at[i, :, p], dst.at[i, :, p], p_send.at[n], p_recv.at[n, i], in_plane(p)).start()
        dst[i, :, 0] = mid[i, :, 0]

    def arrived(n, dst, i):
        wait_bytes(dst.at[i, :, pl.ds(1, PLANE - 1)], p_recv.at[n, i])
        return dst[i].astype(F32).reshape(SLOTS, 128)

    def all_sent(n, src, dst):
        for i in range(PARTS):
            wait_bytes(src.at[i, pl.ds(1, NZ - 1)], z_send.at[n])
            wait_bytes(dst.at[i, :, pl.ds(1, PLANE - 1)], p_send.at[n])

    tags_along_z(0, 1)
    for i in range(PARTS):
        along_z(0, send_a, mid_a, i)
    tags_in_plane(0, 1)
    forward(0, mid_a, recv_a, 0)

    got = in_a_row(tags_got(0)).astype(I32) - 1
    local_b = got >> 12
    code_b = jnp.where(got >= 0, got & 4095, -1)
    half_b = ((z - (iota((1, SLOTS), 1) >> 7)) & (NZ - 1)) >> 2
    key = jnp.where(got >= 0, (code_b >> 4) * 2 + half_b, -1)
    key_f = key.astype(F32)
    key_lines = lines([(key >> 4).astype(F32), (key & 15).astype(F32)], SLOTS)
    weights = lines([16.0, 1.0], SLOTS)
    rank_b = jnp.zeros((1, SLOTS), F32)
    for c in range(NZ):
        key_col = dot(key_lines[:, c * CHUNK : (c + 1) * CHUNK], weights, ((0,), (0,)))
        before = iota((CHUNK, SLOTS), 0) + c * CHUNK < iota((CHUNK, SLOTS), 1)
        hit = jnp.where((key_col == key_f) & before, 1.0, 0.0)
        rank_b += jnp.sum(hit, axis=0, keepdims=True)
    dest_b = offset(code_b >> 5) * CAP + ((code_b >> 4) & 1) * 4 + half_b * 2 + rank_b.astype(I32)
    dest_b = jnp.where(got >= 0, dest_b, -1)
    tags_b = lines([(code_b & 31).astype(F32), 1.0], SLOTS)

    def plan(c, carry):
        pick = one_hot(iota((CHUNK, SLOTS), 0) + c * CHUNK == dest_b)
        pick_b[pl.ds(c * CHUNK, CHUNK), :] = pick
        t = dot(tags_b, pick, ((1,), (1,)))
        tag_send[1, c] = t[0:1] + t[1:2]
        return carry

    lax.fori_loop(0, NZ, plan, 0)
    tags_along_z(1, 1)
    for c in range(NZ):
        pick = one_hot(iota((128, CHUNK), 0) == local_b[:, c * CHUNK : (c + 1) * CHUNK])
        base = dot(pick, coarse_ref[...], ((0,), (0,)))
        base_ref[c * CHUNK : (c + 1) * CHUNK, :] = base.astype(BF16)

    def residual(i):
        at = slice(i * 128, (i + 1) * 128)
        res = (arrived(0, recv_a, i) - base_ref[:, at].astype(F32)).astype(BF16)
        res_full[feat, :, at] = res
        send_b[i] = dot(pick_b[...], res).reshape(NZ, PLANE, CAP, 128).astype(BF16)
        along_z(1, send_b, mid_b, i)

    forward(0, mid_a, recv_a, 1)
    residual(0)
    forward(0, mid_a, recv_a, 2)
    tags_in_plane(1, 1)
    residual(1)
    residual(2)
    swap_res = remote(res_full.at[feat], res_full.at[feat], swap_send.at[0], swap_recv.at[0], sibling)
    swap_res.start()
    forward(1, mid_b, recv_b, 0)

    word = in_a_row(tags_got(1)).astype(I32) - 1
    named = iota((32, SLOTS), 0) == word
    counts = jnp.sum(jnp.where(named, 1.0, 0.0), axis=1, keepdims=True)
    count = jnp.where(feat == 0, counts[:16], counts[16:])
    named = one_hot(named)

    def order(b):
        first, last = ((x, y), (y, x))[b % 2]
        line = (last * 4 + first) * NZ
        return line + z, line, last

    def on(axis, i):
        return chip(0, i, 0) if axis == 0 else chip(0, 0, i)

    def gather_z(b, block):
        at, _, _ = order(b)
        books[b, at] = block
        ref = books.at[b, at]
        for dz in range(1, NZ):
            remote(ref, ref, g_send.at[b, 0], g_recv.at[b, 0], chip(dz, 0, 0)).start()

    def some(b, n):
        return books.at[b, pl.ds(0, n)]

    def gather_line(b):
        wait_bytes(some(b, NZ - 1), g_recv.at[b, 0])
        _, line, _ = order(b)
        ref = books.at[b, pl.ds(line, NZ)]
        for i in (2, 1, 3):
            remote(ref, ref, g_send.at[b, 1], g_recv.at[b, 1], on(1 - b % 2, i)).start()

    def ring(b, k):
        _, _, last = order(b)
        for d, i in enumerate((1, 3)):
            if k == 0:
                ref = books.at[b, pl.ds(last * SLAB, SLAB)]
            else:
                ref = books.at[b, pl.ds(((last - i) & 3) * SLAB + d * (SLAB // 2), SLAB // 2)]
            remote(ref, ref, r_send.at[b, k, d], r_recv.at[b, k, d], on(b % 2, i)).start()

    def gather_ring(b):
        wait_bytes(some(b, 3 * NZ), g_recv.at[b, 1])
        ring(b, 0)

    def ring_came(b, k):
        for d in range(2):
            wait_bytes(some(b, SLAB >> k), r_recv.at[b, k, d])

    def gather_on(b):
        ring_came(b, 0)
        ring(b, 1)

    def both(do, i):
        do(2 * i)
        do(2 * i + 1)

    def update(i):
        sums = dot(named, arrived(1, recv_b, i).astype(BF16))
        sums_own[i, 0], sums_own[i, 1] = sums[:16], sums[16:]
        swap = remote(sums_own.at[i, 1 - feat], sums_sib.at[i], swap_send.at[1 + i], swap_recv.at[1 + i], sibling)
        swap.start()
        mine = jnp.where(feat == 0, sums[:16], sums[16:])
        swap.wait()
        theirs = sums_sib[i]
        block = []
        for f in range(2):
            at = slice(f * HALF + i * 128, f * HALF + (i + 1) * 128)
            total = jnp.where(feat == f, mine, theirs)
            new = (total + PRIOR * codebook_ref[:, at]) / (count + PRIOR)
            updated_ref[:, at] = new
            block.append(new.astype(BF16))
        for f in range(2):
            gather_z(2 * i + f, block[f])

    def rows_side():
        swap_res.wait()
        ones = jnp.ones((16, HALF), BF16)
        norm = jnp.zeros((16, SLOTS), F32)
        for f in range(2):
            r = res_full[f].astype(F32)
            for i in range(PARTS):
                at = i * 2 + f
                row_rhs[:, at * 128 : (at + 1) * 128] = (-2.0 * r[:, i * 128 : (i + 1) * 128]).astype(BF16)
            sq = r * r
            sq_hi = sq.astype(BF16)
            sq_lo = (sq - sq_hi.astype(F32)).astype(BF16)
            norm += dot(ones, sq_hi, ((1,), (1,))) + dot(ones, sq_lo, ((1,), (1,)))
        return norm[0:1]

    forward(1, mid_b, recv_b, 1)
    update(0)
    row_norm = rows_side()
    forward(1, mid_b, recv_b, 2)
    both(gather_line, 0)
    update(1)
    both(gather_ring, 0)
    both(gather_line, 1)
    update(2)
    both(gather_ring, 1)
    both(gather_on, 0)
    both(gather_line, 2)
    both(gather_on, 1)
    both(gather_ring, 2)
    both(lambda b: ring_came(b, 1), 0)
    both(lambda b: ring_came(b, 1), 1)

    def blocks(b, c):
        at = [i if b % 2 == 0 else i % 4 * 4 + i // 4 for i in range(PLANE)]
        return jnp.concatenate([books[b, i * NZ + c] for i in at], axis=0)

    def products(c, pieces):
        piece = jnp.concatenate([blocks(b, c) for b in pieces], axis=1)
        f = piece.astype(F32)
        at = slice(pieces[0] * 128, (pieces[-1] + 1) * 128)
        return dot(piece, row_rhs[:, at], ((1,), (1,))) + jnp.sum(f * f, axis=1, keepdims=True)

    def begin(c, carry):
        acc_ref[c] = products(c, (0, 1, 2, 3))
        return carry

    lax.fori_loop(0, NZ, begin, 0)
    both(gather_on, 2)
    both(lambda b: ring_came(b, 1), 2)

    def book_sent():
        for b in range(2 * PARTS):
            wait_bytes(some(b, NZ - 1), g_send.at[b, 0])
            wait_bytes(some(b, 3 * NZ), g_send.at[b, 1])
            for k in range(2):
                for d in range(2):
                    wait_bytes(some(b, SLAB >> k), r_send.at[b, k, d])


    def finish(c, best):
        dist = acc_ref[c] + products(c, (4, 5))
        return jnp.minimum(best, jnp.min(dist.reshape(32, 8, SLOTS), axis=0))

    best = lax.fori_loop(0, NZ, finish, jnp.full((8, SLOTS), 3e38, F32))
    best = (jnp.min(best, axis=0, keepdims=True) + row_norm) / FEATURES
    for c in range(NZ):
        tag_send[2, c] = best[:, c * CHUNK : (c + 1) * CHUNK]

    tags_along_z(2, -1)
    tags_in_plane(2, -1)
    back = tags_got(2)
    parts = []
    for _ in range(3):
        parts.append(back.astype(BF16).astype(F32))
        back = back - parts[-1]
    lane = one_hot(iota((128, ROWS), 0) == (dest & 127))
    near = dot(jnp.concatenate(parts, axis=0).astype(BF16), lane)
    near = near[:8] + near[8:16] + near[16:]
    near = jnp.sum(jnp.where(iota((NZ, ROWS), 0) == (dest >> 7), near, 0.0), axis=0, keepdims=True)
    near_own[...] = near
    swap_near = remote(near_own, near_sib, swap_send.at[4], swap_recv.at[4], sibling)
    swap_near.start()

    for n in range(3):
        tags_sent(n)
    all_sent(0, send_a, recv_a)
    all_sent(1, send_b, recv_b)
    book_sent()
    swap_near.wait()
    nearest_ref[...] = jnp.minimum(near, near_sib[...])


def per_device(rows, list_ids, code_ids, list_slot, coarse, codebook):
    vmem, hbm = pl.BlockSpec(memory_space=pltpu.VMEM), pl.BlockSpec(memory_space=pl.ANY)
    messages = pltpu.VMEM((PARTS, NZ, PLANE, CAP, 128), BF16)
    dma = pltpu.SemaphoreType.DMA
    updated, nearest = pl.pallas_call(
        kernel,
        out_shape=(
            jax.ShapeDtypeStruct((16, FEATURES), F32),
            jax.ShapeDtypeStruct((1, ROWS), F32),
        ),
        in_specs=[hbm] * 6,
        out_specs=(vmem, vmem),
        scratch_shapes=[
            pltpu.VMEM((ROWS, HALF), BF16),
            pltpu.VMEM((1, ROWS), I32),
            pltpu.VMEM((1, ROWS), I32),
            pltpu.VMEM((128, 128), I32),
            pltpu.VMEM((128, HALF), BF16),
            pltpu.VMEM((16, FEATURES), F32),
            messages, messages, messages, messages, messages, messages,
            pltpu.VMEM((3, NZ, 1, 128), F32),
            pltpu.VMEM((3, NZ, 1, 128), F32),
            pltpu.VMEM((3, PLANE, NZ, 1, 128), F32),
            pltpu.VMEM((SLOTS, SLOTS), BF16),
            pltpu.VMEM((SLOTS, HALF), BF16),
            pltpu.VMEM((2, SLOTS, HALF), BF16),
            pltpu.VMEM((SLOTS, FEATURES), BF16),
            pltpu.VMEM((NZ, 256, SLOTS), F32),
            pltpu.VMEM((PARTS, 2, 16, 128), F32),
            pltpu.VMEM((PARTS, 16, 128), F32),
            pltpu.VMEM((2 * PARTS, CHIPS, 16, 128), BF16),
            pltpu.VMEM((1, ROWS), F32),
            pltpu.VMEM((1, ROWS), F32),
            dma((6,)), dma((2,)), dma((2, PARTS)), dma((2,)), dma((2, PARTS)), dma((3, 4)), dma((5,)), dma((5,)),
            dma((6, 2)), dma((6, 2)), dma((6, 2, 2)), dma((6, 2, 2)),
        ],
        compiler_params=pltpu.CompilerParams(
            collective_id=0, has_side_effects=True, vmem_limit_bytes=63 * 2**20
        ),
    )(
        rows,
        list_ids.reshape(1, ROWS),
        code_ids.reshape(1, ROWS),
        list_slot.reshape(128, 128),
        coarse,
        codebook,
    )
    return updated, nearest.reshape(ROWS)


def solution(mesh):
    placed = (P("rep", "feat"), P("rep"), P("rep"), P(), P("rep", None), P(("rep", "feat"), None))
    return jax.shard_map(
        per_device,
        mesh=mesh,
        in_specs=placed,
        out_specs=(P(("rep", "feat"), None), P("rep")),
        check_vma=False,
    )
```

time: 111 us -> 98.1 us (0.88)
  Pallas kernels: 108 us -> 95.3 us
    pallas_call x1, Pallas kernels: 108 us -> 95.3 us  [per_device(): pl.pallas_call(kernel, out_shape=(jax.ShapeDtypeStruct((16, FEATURES), F3...]
where the time goes in v3:
time: 98.1 us; the launch traced here: 97.9 us
  Pallas kernels  95.3 us (97%)
  local copies, waits for them, and re-layouts  2.01 us (2%)
    pallas_call x1, Pallas kernels, per_device(): pl.pallas_call(kernel, out_shape=(jax.ShapeDtypeStruct((16, FEATURES), F3...  95.3 us
    unnamed x4, local copies, waits for them, and re-layouts  2.01 us

profile of v3, /device:TPU:1, one launch (start us, length us, event | category | flops | bytes accessed | tf_op | source)
XLA Modules:
  0.0 97.9 jit_solution(5921511094153136165)
XLA Ops:
  0.6 95.3 %shard_map.77 = (f32[16,768]{1,0:T(8,128)}, f32[1,512]{1,0:T(1,128)}) custom-call(bf16[512,384]{1,0:T(8,128)(2,1)} %rows_hbm.1, s32[1,512]{1,0:T(1,128)} %bitcast.5, s32[1,512]{1,0:T(1,128)} %bitcast.6, s32[128,128]{1,0:T(8,128)} %bitcast.4, bf16[128,768]{1,0:T(8,128)(2,1)} %coarse_hbm.1, f32[16,768]{1,0:T(8,128)} %codebook_hbm.1), custom_call_target="tpu_custom_call" | custom-call | tf_op jit(solution)/shard_map/pallas_call | solution.py:408
  95.9 0.0 copy-start
  95.9 1.4 %copy.10 = f32[16,768]{1,0:T(8,128)} copy(f32[16,768]{1,0:T(8,128)} %get-tuple-element.8) | data formatting | bytes 98304
  97.3 0.0 copy-done
  97.3 0.6 copy.11
Async XLA Ops:
  95.9 1.4 %copy-start = (f32[1,512]{1,0:T(1,128)S(1)}, f32[1,512]{1,0:T(1,128)}, u32[]{:S(2)}) copy-start(f32[1,512]{1,0:T(1,128)} %get-tuple-element.5) | copy-start | bytes 6148

commit v4 on v3

--- a/solution.py
+++ b/solution.py
@@ -19,6 +19,8 @@
 MESH = pl.DeviceIdType.MESH
 F32, BF16, I32 = jnp.float32, jnp.bfloat16, jnp.int32
 SLAB = 4 * NZ
+FAR_Z = (4, 3, 5, 2, 6, 1, 7)
+FAR_P = (10, 6, 9, 11, 14, 2, 5, 7, 8, 13, 15, 1, 3, 4, 12)
 PARTS = 3
 
 
@@ -80,10 +82,9 @@
     for load in loads:
         load.start()
     barrier = pltpu.get_barrier_semaphore()
-    for p in range(1, PLANE):
-        pl.semaphore_signal(barrier, inc=1, device_id=in_plane(p), device_id_type=MESH)
-    for dz in range(1, NZ):
-        pl.semaphore_signal(barrier, inc=1, device_id=chip(dz, 0, 0), device_id_type=MESH)
+    far = [chip(dz, 0, 0) for dz in FAR_Z] + [in_plane(p) for p in FAR_P]
+    for i in range(PLANE + NZ - 2):
+        pl.semaphore_signal(barrier, inc=1, device_id=far[i // 2 + (i % 2) * 7 if i < 14 else i], device_id_type=MESH)
     pl.semaphore_signal(barrier, inc=1, device_id=sibling, device_id_type=MESH)
 
     for load in loads[:3]:
@@ -133,14 +134,14 @@
     pl.semaphore_wait(barrier, PLANE + NZ - 1)
 
     def tags_along_z(n, sign):
-        for dz in range(1, NZ):
+        for dz in FAR_Z:
             remote(tag_send.at[n, dz], tag_mid.at[n, dz], tag_sem.at[n, 0], tag_sem.at[n, 1],
                    chip(sign * dz, 0, 0)).start()
         tag_mid[n, 0] = tag_send[n, 0]
 
     def tags_in_plane(n, sign):
         wait_bytes(tag_mid.at[n, pl.ds(1, NZ - 1)], tag_sem.at[n, 1])
-        for p in range(1, PLANE):
+        for p in FAR_P:
             remote(tag_mid.at[n], tag_recv.at[n, p], tag_sem.at[n, 2], tag_sem.at[n, 3],
                    in_plane(p, sign)).start()
         tag_recv[n, 0] = tag_mid[n]
@@ -161,13 +162,13 @@
         return jnp.concatenate([t[c : c + 1] for c in range(NZ)], axis=1)
 
     def along_z(n, src, mid, i):
-        for dz in (4, 3, 5, 2, 6, 1, 7):
+        for dz in FAR_Z:
             remote(src.at[i, dz], mid.at[i, dz], z_send.at[n], z_recv.at[n, i], chip(dz, 0, 0)).start()
         mid[i, 0] = src[i, 0]
 
     def forward(n, mid, dst, i):
         wait_bytes(mid.at[i, pl.ds(1, NZ - 1)], z_recv.at[n, i])
-        for p in range(1, PLANE):
+        for p in FAR_P:
             remote(mid.at[i, :, p], dst.at[i, :, p], p_send.at[n], p_recv.at[n, i], in_plane(p)).start()
         dst[i, :, 0] = mid[i, :, 0]
 
@@ -241,6 +242,23 @@
     count = jnp.where(feat == 0, counts[:16], counts[16:])
     named = one_hot(named)
 
+    def rows_side():
+        swap_res.wait()
+        ones = jnp.ones((16, HALF), BF16)
+        norm = jnp.zeros((16, SLOTS), F32)
+        for f in range(2):
+            r = res_full[f].astype(F32)
+            for i in range(PARTS):
+                at = i * 2 + f
+                row_rhs[:, at * 128 : (at + 1) * 128] = (-2.0 * r[:, i * 128 : (i + 1) * 128]).astype(BF16)
+            sq = r * r
+            sq_hi = sq.astype(BF16)
+            sq_lo = (sq - sq_hi.astype(F32)).astype(BF16)
+            norm += dot(ones, sq_hi, ((1,), (1,))) + dot(ones, sq_lo, ((1,), (1,)))
+        return norm[0:1]
+
+    row_norm = rows_side()
+
     def order(b):
         first, last = ((x, y), (y, x))[b % 2]
         line = (last * 4 + first) * NZ
@@ -253,7 +271,7 @@
         at, _, _ = order(b)
         books[b, at] = block
         ref = books.at[b, at]
-        for dz in range(1, NZ):
+        for dz in FAR_Z:
             remote(ref, ref, g_send.at[b, 0], g_recv.at[b, 0], chip(dz, 0, 0)).start()
 
     def some(b, n):
@@ -278,6 +296,13 @@
     def gather_ring(b):
         wait_bytes(some(b, 3 * NZ), g_recv.at[b, 1])
         ring(b, 0)
+
+    def slab_direct(b):
+        wait_bytes(some(b, 3 * NZ), g_recv.at[b, 1])
+        _, _, last = order(b)
+        ref = books.at[b, pl.ds(last * SLAB, SLAB)]
+        for i in (2, 1, 3):
+            remote(ref, ref, r_send.at[b, 0, 0], r_recv.at[b, 0, 0], on(b % 2, i)).start()
 
     def ring_came(b, k):
         for d in range(2):
@@ -309,35 +334,19 @@
         for f in range(2):
             gather_z(2 * i + f, block[f])
 
-    def rows_side():
-        swap_res.wait()
-        ones = jnp.ones((16, HALF), BF16)
-        norm = jnp.zeros((16, SLOTS), F32)
-        for f in range(2):
-            r = res_full[f].astype(F32)
-            for i in range(PARTS):
-                at = i * 2 + f
-                row_rhs[:, at * 128 : (at + 1) * 128] = (-2.0 * r[:, i * 128 : (i + 1) * 128]).astype(BF16)
-            sq = r * r
-            sq_hi = sq.astype(BF16)
-            sq_lo = (sq - sq_hi.astype(F32)).astype(BF16)
-            norm += dot(ones, sq_hi, ((1,), (1,))) + dot(ones, sq_lo, ((1,), (1,)))
-        return norm[0:1]
-
     forward(1, mid_b, recv_b, 1)
     update(0)
-    row_norm = rows_side()
     forward(1, mid_b, recv_b, 2)
     both(gather_line, 0)
     update(1)
     both(gather_ring, 0)
+    update(2)
     both(gather_line, 1)
-    update(2)
+    both(gather_on, 0)
     both(gather_ring, 1)
-    both(gather_on, 0)
     both(gather_line, 2)
     both(gather_on, 1)
-    both(gather_ring, 2)
+    both(slab_direct, 2)
     both(lambda b: ring_came(b, 1), 0)
     both(lambda b: ring_came(b, 1), 1)
 
@@ -356,23 +365,27 @@
         return carry
 
     lax.fori_loop(0, NZ, begin, 0)
-    both(gather_on, 2)
-    both(lambda b: ring_came(b, 1), 2)
+    both(lambda b: wait_bytes(some(b, 3 * SLAB), r_recv.at[b, 0, 0]), 2)
 
     def book_sent():
         for b in range(2 * PARTS):
             wait_bytes(some(b, NZ - 1), g_send.at[b, 0])
             wait_bytes(some(b, 3 * NZ), g_send.at[b, 1])
+            if b >= 4:
+                wait_bytes(some(b, 3 * SLAB), r_send.at[b, 0, 0])
+                continue
             for k in range(2):
                 for d in range(2):
                     wait_bytes(some(b, SLAB >> k), r_send.at[b, k, d])
 
 
     def finish(c, best):
-        dist = acc_ref[c] + products(c, (4, 5))
-        return jnp.minimum(best, jnp.min(dist.reshape(32, 8, SLOTS), axis=0))
-
-    best = lax.fori_loop(0, NZ, finish, jnp.full((8, SLOTS), 3e38, F32))
+        for i in range(2):
+            dist = acc_ref[2 * c + i] + products(2 * c + i, (4, 5))
+            best = jnp.minimum(best, jnp.min(dist.reshape(32, 8, SLOTS), axis=0))
+        return best
+
+    best = lax.fori_loop(0, NZ // 2, finish, jnp.full((8, SLOTS), 3e38, F32))
     best = (jnp.min(best, axis=0, keepdims=True) + row_norm) / FEATURES
     for c in range(NZ):
         tag_send[2, c] = best[:, c * CHUNK : (c + 1) * CHUNK]

time: 98.1 us -> 91.5 us (0.933)
  Pallas kernels: 95.3 us -> 88.7 us
    pallas_call x1, Pallas kernels: 95.3 us -> 88.7 us  [per_device(): pl.pallas_call(kernel, out_shape=(jax.ShapeDtypeStruct((16, FEATURES), F3...]
where the time goes in v4:
time: 91.5 us; the launch traced here: 91.3 us
  Pallas kernels  88.7 us (97%)
  local copies, waits for them, and re-layouts  2.01 us (2%)
    pallas_call x1, Pallas kernels, per_device(): pl.pallas_call(kernel, out_shape=(jax.ShapeDtypeStruct((16, FEATURES), F3...  88.7 us
    unnamed x4, local copies, waits for them, and re-layouts  2.01 us

profile of v4, /device:TPU:1, one launch (start us, length us, event | category | flops | bytes accessed | tf_op | source)
XLA Modules:
  0.0 91.3 jit_solution(1533796260159236879)
XLA Ops:
  0.6 88.7 %shard_map.77 = (f32[16,768]{1,0:T(8,128)}, f32[1,512]{1,0:T(1,128)}) custom-call(bf16[512,384]{1,0:T(8,128)(2,1)} %rows_hbm.1, s32[1,512]{1,0:T(1,128)} %bitcast.5, s32[1,512]{1,0:T(1,128)} %bitcast.6, s32[128,128]{1,0:T(8,128)} %bitcast.4, bf16[128,768]{1,0:T(8,128)(2,1)} %coarse_hbm.1, f32[16,768]{1,0:T(8,128)} %codebook_hbm.1), custom_call_target="tpu_custom_call" | custom-call | tf_op jit(solution)/shard_map/pallas_call | solution.py:421
  89.3 0.0 copy-start
  89.3 1.4 %copy.10 = f32[16,768]{1,0:T(8,128)} copy(f32[16,768]{1,0:T(8,128)} %get-tuple-element.8) | data formatting | bytes 98304
  90.7 0.0 copy-done
  90.7 0.6 copy.11
Async XLA Ops:
  89.3 1.4 %copy-start = (f32[1,512]{1,0:T(1,128)S(1)}, f32[1,512]{1,0:T(1,128)}, u32[]{:S(2)}) copy-start(f32[1,512]{1,0:T(1,128)} %get-tuple-element.5) | copy-start | bytes 6148

commit v5 on v4

--- a/solution.py
+++ b/solution.py
@@ -250,7 +250,7 @@
             r = res_full[f].astype(F32)
             for i in range(PARTS):
                 at = i * 2 + f
-                row_rhs[:, at * 128 : (at + 1) * 128] = (-2.0 * r[:, i * 128 : (i + 1) * 128]).astype(BF16)
+                row_rhs[at * 128 : (at + 1) * 128, :] = (-2.0 * r[:, i * 128 : (i + 1) * 128]).T.astype(BF16)
             sq = r * r
             sq_hi = sq.astype(BF16)
             sq_lo = (sq - sq_hi.astype(F32)).astype(BF16)
@@ -355,16 +355,18 @@
         return jnp.concatenate([books[b, i * NZ + c] for i in at], axis=0)
 
     def products(c, pieces):
-        piece = jnp.concatenate([blocks(b, c) for b in pieces], axis=1)
+        piece = jnp.concatenate(
+            [jnp.concatenate([blocks(b, 2 * c + i) for b in pieces], axis=1) for i in range(2)], axis=0
+        )
         f = piece.astype(F32)
         at = slice(pieces[0] * 128, (pieces[-1] + 1) * 128)
-        return dot(piece, row_rhs[:, at], ((1,), (1,))) + jnp.sum(f * f, axis=1, keepdims=True)
+        return dot(piece, row_rhs[at, :]) + jnp.sum(f * f, axis=1, keepdims=True)
 
     def begin(c, carry):
         acc_ref[c] = products(c, (0, 1, 2, 3))
         return carry
 
-    lax.fori_loop(0, NZ, begin, 0)
+    lax.fori_loop(0, NZ // 2, begin, 0)
     both(lambda b: wait_bytes(some(b, 3 * SLAB), r_recv.at[b, 0, 0]), 2)
 
     def book_sent():
@@ -380,10 +382,8 @@
 
 
     def finish(c, best):
-        for i in range(2):
-            dist = acc_ref[2 * c + i] + products(2 * c + i, (4, 5))
-            best = jnp.minimum(best, jnp.min(dist.reshape(32, 8, SLOTS), axis=0))
-        return best
+        dist = acc_ref[c] + products(c, (4, 5))
+        return jnp.minimum(best, jnp.min(dist.reshape(64, 8, SLOTS), axis=0))
 
     best = lax.fori_loop(0, NZ // 2, finish, jnp.full((8, SLOTS), 3e38, F32))
     best = (jnp.min(best, axis=0, keepdims=True) + row_norm) / FEATURES
@@ -440,8 +440,8 @@
             pltpu.VMEM((SLOTS, SLOTS), BF16),
             pltpu.VMEM((SLOTS, HALF), BF16),
             pltpu.VMEM((2, SLOTS, HALF), BF16),
-            pltpu.VMEM((SLOTS, FEATURES), BF16),
-            pltpu.VMEM((NZ, 256, SLOTS), F32),
+            pltpu.VMEM((FEATURES, SLOTS), BF16),
+            pltpu.VMEM((NZ // 2, 512, SLOTS), F32),
             pltpu.VMEM((PARTS, 2, 16, 128), F32),
             pltpu.VMEM((PARTS, 16, 128), F32),
             pltpu.VMEM((2 * PARTS, CHIPS, 16, 128), BF16),

time: 91.5 us -> 90.3 us (0.987)
  Pallas kernels: 88.7 us -> 87.5 us
    pallas_call x1, Pallas kernels: 88.7 us -> 87.5 us  [per_device(): pl.pallas_call(kernel, out_shape=(jax.ShapeDtypeStruct((16, FEATURES), F3...]
where the time goes in v5:
time: 90.3 us; the launch traced here: 90.2 us
  Pallas kernels  87.5 us (97%)
  local copies, waits for them, and re-layouts  2.01 us (2%)
    pallas_call x1, Pallas kernels, per_device(): pl.pallas_call(kernel, out_shape=(jax.ShapeDtypeStruct((16, FEATURES), F3...  87.5 us
    unnamed x4, local copies, waits for them, and re-layouts  2.01 us

profile of v5, /device:TPU:1, one launch (start us, length us, event | category | flops | bytes accessed | tf_op | source)
XLA Modules:
  0.0 90.2 jit_solution(15442672085730197551)
XLA Ops:
  0.6 87.5 %shard_map.77 = (f32[16,768]{1,0:T(8,128)}, f32[1,512]{1,0:T(1,128)}) custom-call(bf16[512,384]{1,0:T(8,128)(2,1)} %rows_hbm.1, s32[1,512]{1,0:T(1,128)} %bitcast.5, s32[1,512]{1,0:T(1,128)} %bitcast.6, s32[128,128]{1,0:T(8,128)} %bitcast.4, bf16[128,768]{1,0:T(8,128)(2,1)} %coarse_hbm.1, f32[16,768]{1,0:T(8,128)} %codebook_hbm.1), custom_call_target="tpu_custom_call" | custom-call | tf_op jit(solution)/shard_map/pallas_call | solution.py:421
  88.2 0.0 copy-start
  88.2 1.4 %copy.10 = f32[16,768]{1,0:T(8,128)} copy(f32[16,768]{1,0:T(8,128)} %get-tuple-element.8) | data formatting | bytes 98304
  89.6 0.0 copy-done
  89.6 0.6 copy.11
Async XLA Ops:
  88.2 1.4 %copy-start = (f32[1,512]{1,0:T(1,128)S(1)}, f32[1,512]{1,0:T(1,128)}, u32[]{:S(2)}) copy-start(f32[1,512]{1,0:T(1,128)} %get-tuple-element.5) | copy-start | bytes 6148

commit v6 on v5

--- a/solution.py
+++ b/solution.py
@@ -42,7 +42,7 @@
     rows_ref, lid_ref, code_ref, table_ref, coarse_ref, codebook_ref,
     send_a, mid_a, recv_a, send_b, mid_b, recv_b,
     tag_send, tag_mid, tag_recv, pick_b, base_ref, res_full, row_rhs, acc_ref,
-    sums_own, sums_sib, books, near_own, near_sib,
+    sums_own, sums_sib, books, min_mid,
     load_sem, z_send, z_recv, p_send, p_recv, tag_sem, swap_send, swap_recv, g_send, g_recv, r_send, r_recv,
 ):
     rep, feat = lax.axis_index("rep"), lax.axis_index("feat")
@@ -82,8 +82,10 @@
     for load in loads:
         load.start()
     barrier = pltpu.get_barrier_semaphore()
+    across = [(chip(dz, 0, 0)[0], 1 - feat) for dz in FAR_Z]
     far = [chip(dz, 0, 0) for dz in FAR_Z] + [in_plane(p) for p in FAR_P]
-    for i in range(PLANE + NZ - 2):
+    far += across
+    for i in range(PLANE + 2 * NZ - 3):
         pl.semaphore_signal(barrier, inc=1, device_id=far[i // 2 + (i % 2) * 7 if i < 14 else i], device_id_type=MESH)
     pl.semaphore_signal(barrier, inc=1, device_id=sibling, device_id_type=MESH)
 
@@ -131,7 +133,7 @@
     lax.fori_loop(0, NZ, pack_rows, 0)
     loads[4].wait()
     loads[5].wait()
-    pl.semaphore_wait(barrier, PLANE + NZ - 1)
+    pl.semaphore_wait(barrier, PLANE + 2 * NZ - 2)
 
     def tags_along_z(n, sign):
         for dz in FAR_Z:
@@ -390,8 +392,23 @@
     for c in range(NZ):
         tag_send[2, c] = best[:, c * CHUNK : (c + 1) * CHUNK]
 
-    tags_along_z(2, -1)
-    tags_in_plane(2, -1)
+    min_mid[feat, 0] = best[:, :CHUNK]
+    for dz in FAR_Z:
+        to = chip(-dz, 0, 0)
+        remote(tag_send.at[2, dz], min_mid.at[feat, dz], tag_sem.at[2, 0], tag_sem.at[2, 1], to).start()
+        remote(tag_send.at[2, dz], min_mid.at[feat, dz], swap_send.at[4], swap_recv.at[4], (to[0], 1 - feat)).start()
+    remote(tag_send.at[2, 0], min_mid.at[feat, 0], swap_send.at[4], swap_recv.at[4], sibling).start()
+    for n in range(2):
+        tags_sent(n)
+    all_sent(0, send_a, recv_a)
+    all_sent(1, send_b, recv_b)
+    book_sent()
+    wait_bytes(min_mid.at[0, pl.ds(1, NZ - 1)], tag_sem.at[2, 1])
+    wait_bytes(min_mid.at[0], swap_recv.at[4])
+    tag_mid[2] = jnp.minimum(min_mid[0], min_mid[1])
+    for p in FAR_P:
+        remote(tag_mid.at[2], tag_recv.at[2, p], tag_sem.at[2, 2], tag_sem.at[2, 3], in_plane(p, -1)).start()
+    tag_recv[2, 0] = tag_mid[2]
     back = tags_got(2)
     parts = []
     for _ in range(3):
@@ -401,17 +418,9 @@
     near = dot(jnp.concatenate(parts, axis=0).astype(BF16), lane)
     near = near[:8] + near[8:16] + near[16:]
     near = jnp.sum(jnp.where(iota((NZ, ROWS), 0) == (dest >> 7), near, 0.0), axis=0, keepdims=True)
-    near_own[...] = near
-    swap_near = remote(near_own, near_sib, swap_send.at[4], swap_recv.at[4], sibling)
-    swap_near.start()
-
-    for n in range(3):
-        tags_sent(n)
-    all_sent(0, send_a, recv_a)
-    all_sent(1, send_b, recv_b)
-    book_sent()
-    swap_near.wait()
-    nearest_ref[...] = jnp.minimum(near, near_sib[...])
+    nearest_ref[...] = near
+    tags_sent(2)
+    wait_bytes(min_mid.at[0], swap_send.at[4])
 
 
 def per_device(rows, list_ids, code_ids, list_slot, coarse, codebook):
@@ -445,8 +454,7 @@
             pltpu.VMEM((PARTS, 2, 16, 128), F32),
             pltpu.VMEM((PARTS, 16, 128), F32),
             pltpu.VMEM((2 * PARTS, CHIPS, 16, 128), BF16),
-            pltpu.VMEM((1, ROWS), F32),
-            pltpu.VMEM((1, ROWS), F32),
+            pltpu.VMEM((2, NZ, 1, 128), F32),
             dma((6,)), dma((2,)), dma((2, PARTS)), dma((2,)), dma((2, PARTS)), dma((3, 4)), dma((5,)), dma((5,)),
             dma((6, 2)), dma((6, 2)), dma((6, 2, 2)), dma((6, 2, 2)),
         ],

time: 90.3 us -> 89.8 us (level)
  no operation moved by 1% of the time
where the time goes in v6:
time: 89.8 us; the launch traced here: 89.6 us
  Pallas kernels  87 us (97%)
  local copies, waits for them, and re-layouts  2.01 us (2%)
    pallas_call x1, Pallas kernels, per_device(): pl.pallas_call(kernel, out_shape=(jax.ShapeDtypeStruct((16, FEATURES), F3...  87 us
    unnamed x4, local copies, waits for them, and re-layouts  2.01 us

profile of v6, /device:TPU:1, one launch (start us, length us, event | category | flops | bytes accessed | tf_op | source)
XLA Modules:
  0.0 89.6 jit_solution(4949225488891957924)
XLA Ops:
  0.6 87.0 %shard_map.77 = (f32[16,768]{1,0:T(8,128)}, f32[1,512]{1,0:T(1,128)}) custom-call(bf16[512,384]{1,0:T(8,128)(2,1)} %rows_hbm.1, s32[1,512]{1,0:T(1,128)} %bitcast.5, s32[1,512]{1,0:T(1,128)} %bitcast.6, s32[128,128]{1,0:T(8,128)} %bitcast.4, bf16[128,768]{1,0:T(8,128)(2,1)} %coarse_hbm.1, f32[16,768]{1,0:T(8,128)} %codebook_hbm.1), custom_call_target="tpu_custom_call" | custom-call | tf_op jit(solution)/shard_map/pallas_call | solution.py:430
  87.6 0.0 copy-start
  87.6 1.4 %copy.10 = f32[16,768]{1,0:T(8,128)} copy(f32[16,768]{1,0:T(8,128)} %get-tuple-element.8) | data formatting | bytes 98304
  89.0 0.0 copy-done
  89.0 0.6 copy.11
Async XLA Ops:
  87.6 1.4 %copy-start = (f32[1,512]{1,0:T(1,128)S(1)}, f32[1,512]{1,0:T(1,128)}, u32[]{:S(2)}) copy-start(f32[1,512]{1,0:T(1,128)} %get-tuple-element.5) | copy-start | bytes 6148
